TPU v7x, 512 devices: a whole 4x8x8 slice. The times are simulated.
512 devices in a mesh: band: 16 (over x, y_hi, core), fft: 32 (over y_lo, z).
Axes of the slice: x: 4, y: 8 (y_hi: 2, y_lo: 4; y = y_hi * 4 + y_lo), z: 8, core: 2. Of those that a mesh axis runs over, the one named last changes fastest.
Arguments:
- orbitals: float32 [32, 128, 128, 128], P('band', 'fft'), may hold values from -6 to 6
- mask: int32 [128, 128, 128], P(None, 'fft'), may hold values from 0 to 1, as said below
Outputs:
- exchange: float32 [32, 128, 128, 128], P('band', 'fft')
Inputs may be any that keep to these rules, and one draw needn't show every extreme that they name: mask is symmetric under negation of the frequency: mask[a, b, c] = mask[(-a) mod 128, (-b) mod 128, (-c) mod 128]; it is 0 wherever f(a)^2 + f(b)^2 + f(c)^2 exceeds 128^2 / 4.
All inputs are finite; a program needn't handle non-finite values.
Results may differ from a plain program's by a relative error of at most 0.00013.
Values sent between devices are 32-bit elements; how exact they have to be, the bound alone decides.
No kernel may reach another device: no remote copies, remote signals or barrier semaphores. Data moves between devices by JAX's collectives and lax.ppermute only.
A program may use at most 64 MiB of HBM per device.

v0:
```python
import functools
import math

import jax
import jax.numpy as jnp
import ml_dtypes
import numpy as np
from jax import lax
from jax.experimental import pallas as pl
from jax.experimental.pallas import tpu as pltpu
from jax.sharding import PartitionSpec as P

NG = 128
HALF = NG // 2
N_FFT = 32
SLAB = NG // N_FFT
BLOCK = 2 * SLAB
LANES = 128
ROWS_ALL = 4 * 2 * NG
NO_LINE = 999
VMEM_LIMIT = 20 * 1024 * 1024


def kept(ky):
    return min(HALF, math.isqrt(HALF * HALF - ky * ky) + 1)


def row_sets():
    order = sorted(range(-HALF, HALF), key=lambda k: (abs(k), -k))
    return [order[:32], order[32:64], order[64:96], order[:95:-1]]


KY = row_sets()
WIDE = [max(kept(k) for k in KY[0]), max(kept(k) for k in KY[1])]
SHARED = max(kept(a) + kept(b) for a, b in zip(KY[2], KY[3]))


def layout(count):
    if count == 3:
        rest = NG // 2 - WIDE[1]
        tail = 3 * SHARED - 2 * LANES
        assert 0 <= tail <= rest
        pieces = [(0, f, 0, WIDE[0], HALF * f) for f in range(3)]
        pieces += [(1, 2, 0, WIDE[1], 3 * HALF), (2, 2, SHARED - tail, tail, 3 * HALF + WIDE[1])]
        pieces += [(1, f, 0, WIDE[1], 4 * HALF + HALF * f) for f in range(2)]
        start = 6 * HALF
        pieces += [(2, f, 0, SHARED - (tail if f == 2 else 0), start + SHARED * f) for f in range(3)]
        size = start + 2 * LANES
    else:
        pieces = [(0, f, 0, WIDE[0], HALF * f) for f in range(4)]
        pieces += [(1, f, 0, WIDE[1], HALF * (4 + f)) for f in range(4)]
        pieces += [(2, f, 0, SHARED, 8 * HALF + 96 * f) for f in range(4)]
        size = 7 * LANES
    cut = []
    for kind, field, first, lanes, place in pieces:
        while lanes:
            step = min(lanes, LANES - place % LANES)
            cut.append((kind, field, first, step, place))
            first, lanes, place = first + step, lanes - step, place + step
    return cut, size


@functools.lru_cache(None)
def lane_rows(count):
    pieces, size = layout(count)
    out = np.full((8, size), NO_LINE, np.int32)
    for kind, _, first, lanes, place in pieces:
        spots = np.arange(lanes)
        out[kind, place + spots] = first + spots
        if kind == 2:
            out[3, place + spots] = SHARED - 1 - first - spots
    return out


def turn(a, b):
    angle = (np.asarray(a)[:, None] * np.asarray(b)[None, :]) % NG * (2.0 * np.pi / NG)
    return np.cos(angle), np.sin(angle)


def pair(table):
    high = table.astype(np.float32).astype(ml_dtypes.bfloat16)
    low = (table - high.astype(np.float64)).astype(np.float32).astype(ml_dtypes.bfloat16)
    return np.stack([high, low])


POINTS = np.arange(NG)


@functools.lru_cache(None)
def y_table():
    cosine, sine = turn(np.concatenate(KY), POINTS)
    return np.stack([cosine, -sine], 1).reshape(2 * NG, NG)


def doubled(block):
    return np.kron(np.eye(2), block)


@functools.lru_cache(None)
def z_ahead():
    out = []
    for kz in (np.arange(HALF), np.arange(HALF)[::-1]):
        cosine, sine = turn(POINTS, kz)
        out.append(np.concatenate([doubled(cosine), doubled(sine)], 1))
    return np.concatenate(out, 0)


@functools.lru_cache(None)
def z_back():
    out = []
    for kz in (np.arange(HALF), np.arange(HALF)[::-1]):
        cosine, sine = turn(kz, POINTS)
        weight = np.where(kz == 0, 1.0, 2.0)[:, None]
        cosine, sine = weight * cosine, weight * sine
        sine[kz == 0] = -(1.0 - 2.0 * (POINTS % 2))
        out.append(np.concatenate([doubled(cosine), doubled(sine)], 0))
    return np.concatenate(out, 0)


@functools.lru_cache(None)
def x_tables():
    cosine, sine = turn(POINTS, POINTS)
    ahead = np.zeros((2, NG, N_FFT, 2, SLAB))
    split_planes = lambda table: table.reshape(NG, N_FFT, SLAB)
    ahead[0, :, :, 0] = split_planes(cosine)
    ahead[0, :, :, 1] = split_planes(sine)
    ahead[1, :, :, 0] = split_planes(-sine)
    ahead[1, :, :, 1] = split_planes(cosine)
    ahead = ahead.reshape(2 * NG, 2 * NG)
    return np.concatenate([ahead, ahead.T], 0)


@functools.lru_cache(None)
def mask_rounds():
    edges = {source: [] for source in range(N_FFT)}
    for device in range(N_FFT):
        for rows in range(4):
            index = KY[rows][device] % NG
            edges[index // SLAB].append((device, index % SLAB, rows))
    rounds = []
    for _ in range(SLAB):
        taken = {}

        def place(source, seen):
            for edge in edges[source]:
                if edge[0] in seen:
                    continue
                seen.add(edge[0])
                if edge[0] not in taken or place(taken[edge[0]][0], seen):
                    taken[edge[0]] = (source, edge)
                    return True
            return False

        for source in range(N_FFT):
            assert place(source, set())
        pairs, local, slot = [], [0] * N_FFT, [0] * N_FFT
        for device, (source, edge) in taken.items():
            edges[source].remove(edge)
            pairs.append((source, device))
            local[source] = edge[1]
            slot[device] = edge[2]
        rounds.append((tuple(sorted(pairs)), tuple(local), tuple(slot)))
    return tuple(rounds)


@functools.lru_cache(None)
def device_table():
    out = np.zeros((N_FFT, 16), np.int32)
    for turn_, (_, local, slot) in enumerate(mask_rounds()):
        for device in range(N_FFT):
            ky = KY[slot[device]][device]
            out[device, turn_] = local[device]
            out[device, 4 + turn_] = kept(ky)
            out[device, 8 + turn_] = ky
            out[device, 12 + turn_] = slot[device]
    return out.reshape(-1)


ZERO_ROUND = [slot[0] for _, _, slot in mask_rounds()].index(0)


@functools.lru_cache(None)
def shared_width():
    width = np.repeat(np.asarray([kept(k) for k in KY[2]], np.int32), BLOCK)
    return np.ascontiguousarray(np.broadcast_to(width[:, None], (2 * NG, LANES)))


def split(value):
    high = value.astype(jnp.bfloat16)
    return high, (value - high.astype(jnp.float32)).astype(jnp.bfloat16)


def dot(left, right):
    return jnp.dot(left, right, preferred_element_type=jnp.float32)


def dot3(left, right):
    return dot(left[0], right[0]) + (dot(left[1], right[0]) + dot(left[0], right[1]))


def both(ref, start=0, size=None):
    size = ref.shape[1] if size is None else size
    return ref[0, start : start + size, :], ref[1, start : start + size, :]


def lane_roll(value, shift):
    shift %= LANES
    return value if shift == 0 else pltpu.roll(value, shift, 1)


def parts_swapped(value):
    blocks = value.reshape(-1, BLOCK, value.shape[1])
    return pltpu.roll(blocks, SLAB, 1).reshape(value.shape)


def beside(parts):
    return parts[0] if len(parts) == 1 else jnp.concatenate(parts, axis=1)


def iota(shape, dim):
    return lax.broadcasted_iota(jnp.int32, shape, dim)


def ahead_body(count, products_of, n_in, *refs):
    inputs = refs[:n_in]
    y_ref, z_ref, width_ref, out_ref, *grids = refs[n_in:]
    pieces, size = layout(count)
    fields = products_of(inputs)
    is_imag = iota((2 * NG, LANES), 0) % BLOCK >= SLAB
    sides = {}
    table = both(y_ref)
    for first in range(0, count, 2):
        two = range(first, min(first + 2, count))
        for x in range(SLAB):
            plane = slice(NG * x, NG * x + NG)
            cells = [fields[field](plane) for field in two]
            lines = dot3(table, split(beside(cells)))
            for spot, field in enumerate(two):
                piece = lines[:, NG * spot : NG * (spot + 1)]
                grids[field][pl.ds(x, 2 * NG, stride=SLAB), :] = piece
        for rows in range(4):
            block = slice(2 * NG * rows, 2 * NG * (rows + 1))
            lines = split(beside([grids[field][block, :] for field in two]))
            lines = dot3(lines, both(z_ref, 2 * NG if rows == 3 else 0, NG * len(two)))
            turned = parts_swapped(lines[:, LANES:])
            sides[first // 2, rows] = lines[:, :LANES] + jnp.where(is_imag, -turned, turned)
    lane = iota((2 * NG, LANES), 1)
    shared = {}
    for field in range(count):
        shift = HALF * (field % 2)
        wide = lane_roll(sides[field // 2, 2], -shift)
        narrow = lane_roll(sides[field // 2, 3], SHARED - HALF - shift)
        shared[field] = jnp.where(lane < width_ref[...], wide, narrow)
    tiles = [None] * (size // LANES)
    for kind, field, first, lanes, place in pieces:
        if kind == 2:
            value, shift = shared[field], 0
        else:
            value, shift = sides[field // 2, kind], HALF * (field % 2)
        start = place % LANES
        value = lane_roll(value, start - first - shift)
        old = tiles[place // LANES]
        if old is None:
            old = jnp.zeros_like(value)
        tiles[place // LANES] = jnp.where((lane >= start) & (lane < start + lanes), value, old)
    for tile, value in enumerate(tiles):
        out_ref[:, LANES * tile : LANES * (tile + 1)] = value
    row, column = iota((BLOCK, LANES), 0), iota((BLOCK, LANES), 1)
    sign = (1 - 2 * (iota((1, NG), 1) % 2)).astype(jnp.float32)
    for kind, field, _, _, place in pieces:
        if kind:
            continue
        extra = jnp.zeros((BLOCK, LANES), jnp.float32)
        for x in range(SLAB):
            cells = fields[field](slice(NG * x, NG * x + NG))
            cells = jnp.sum(cells, axis=0, keepdims=True) * sign
            value = jnp.sum(cells, axis=1, keepdims=True)
            extra = jnp.where((row == SLAB + x) & (column == place % LANES), value, extra)
        tile = place // LANES * LANES
        out_ref[0:BLOCK, tile : tile + LANES] += extra


def middle_body(me_ref, device_ref, x_ref, lane_ref, table_ref, *rest):
    *mask_refs, out_ref = rest
    size = x_ref.shape[1]
    base = me_ref[0] * 16
    masks = [ref[...].astype(jnp.float32).astype(jnp.bfloat16) for ref in mask_refs]
    zero_mask = mask_refs[ZERO_ROUND][0:1, HALF : HALF + 1].astype(jnp.float32)
    is_imag = iota((2 * NG, LANES), 0) % BLOCK >= SLAB
    kx = iota((NG, LANES), 0)
    signed = jnp.where(kx < HALF, kx, kx - NG)
    forward = both(table_ref, 0, 2 * NG)
    inverse = both(table_ref, 2 * NG, 2 * NG)
    special = zero_mask / ((1.0 + HALF * HALF / (NG * NG / 16.0)) * float(NG**3))
    for step in range(0, size, 2 * LANES):
        values, real, imag = [], [], []
        for start in range(step, min(step + 2 * LANES, size), LANES):
            lanes = slice(start, start + LANES)
            value = x_ref[:, lanes]
            zero = (lane_ref[0:1, lanes] == 0) & (me_ref[0] == 0)
            mean = jnp.sum(jnp.where(is_imag, value, 0.0), axis=0, keepdims=True) * (1.0 / NG)
            values.append(jnp.where(is_imag & zero, mean, value))
            cells = jnp.zeros((NG, LANES), jnp.float32)
            squared = jnp.zeros((1, LANES), jnp.int32)
            for turn_ in range(4):
                slot = device_ref[base + 12 + turn_]
                kz = lane_ref[0:1, lanes]
                for which in range(1, 4):
                    kz = jnp.where(slot == which, lane_ref[which : which + 1, lanes], kz)
                ky = device_ref[base + 8 + turn_]
                chosen = kz < device_ref[base + 4 + turn_]
                spread = jnp.where((kx == kz) & chosen, 1.0, 0.0).astype(jnp.bfloat16)
                cells += dot(masks[turn_], spread)
                squared += jnp.where(chosen, kz * kz + ky * ky, 0)
            squared = (signed * signed + squared).astype(jnp.float32)
            weight = cells / ((1.0 + squared / (NG * NG / 16.0)) * float(NG**3))
            real.append(weight)
            imag.append(jnp.where((kx == 0) & zero, special, weight))
        spectrum = dot3(forward, split(beside(values)))
        weight = jnp.concatenate([beside(real), beside(imag)], axis=0)
        width = LANES * len(values)
        out_ref[:, step : step + width] = dot3(inverse, split(spectrum * weight))


def potentials(count, lines_ref, y_ref, z_ref, width_ref, grids):
    pieces, _ = layout(count)
    lane = iota((2 * NG, LANES), 1)
    is_imag = iota((2 * NG, LANES), 0) % BLOCK >= SLAB
    sides = {}

    def add(key, value):
        sides[key] = value if key not in sides else sides[key] + value

    shared = {}
    for kind, field, first, lanes, place in pieces:
        tile = place // LANES * LANES
        start = place % LANES
        value = lines_ref[:, tile : tile + LANES]
        value = jnp.where((lane >= start) & (lane < start + lanes), value, 0.0)
        shift = first - start
        if kind == 2:
            value = lane_roll(value, shift)
            shared[field] = value if field not in shared else shared[field] + value
        else:
            add((field // 2, kind), lane_roll(value, shift + HALF * (field % 2)))
    for field, value in shared.items():
        shift = HALF * (field % 2)
        wide = lane < width_ref[...]
        add((field // 2, 2), lane_roll(jnp.where(wide, value, 0.0), shift))
        add((field // 2, 3), lane_roll(jnp.where(wide, 0.0, value), HALF - SHARED + shift))
    for (index, rows), value in sides.items():
        turned = parts_swapped(value)
        value = jnp.concatenate([value, jnp.where(is_imag, turned, -turned)], axis=1)
        table = both(z_ref, 2 * NG if rows == 3 else 0, 2 * NG)
        cells = dot3(split(value), table)
        for field in range(2 * index, min(2 * index + 2, count)):
            block = slice(2 * NG * rows, 2 * NG * (rows + 1))
            grids[field][block, :] = cells[:, NG * (field % 2) : NG * (field % 2 + 1)]
    table = both(y_ref)

    def plane_of(x):
        out = []
        for first in range(0, count, 2):
            two = grids[first : first + 2]
            lines = beside([ref[pl.ds(x, 2 * NG, stride=SLAB), :] for ref in two])
            cells = dot3(table, split(lines))
            out += [cells[:, NG * spot : NG * (spot + 1)] for spot in range(len(two))]
        return out

    return plane_of


def back_own_body(own_ref, lines_ref, y_ref, z_ref, width_ref, out_ref, *grids):
    plane_of = potentials(3, lines_ref, y_ref, z_ref, width_ref, grids)
    for x in range(SLAB):
        plane = slice(NG * x, NG * x + NG)
        first, mixed, second = plane_of(x)
        out_ref[0, plane, :] = first * own_ref[0, plane, :] + mixed * own_ref[1, plane, :]
        out_ref[1, plane, :] = mixed * own_ref[0, plane, :] + second * own_ref[1, plane, :]


def back_cross_body(other_ref, sum_ref, lines_ref, y_ref, z_ref, width_ref, out_ref, *grids):
    plane_of = potentials(4, lines_ref, y_ref, z_ref, width_ref, grids)
    for x in range(SLAB):
        plane = slice(NG * x, NG * x + NG)
        cells = plane_of(x)
        for band in range(2):
            total = cells[2 * band] * other_ref[0, plane, :]
            total += cells[2 * band + 1] * other_ref[1, plane, :]
            out_ref[band, plane, :] = -0.5 * (sum_ref[band, plane, :] + total)


def product(left, i, right, j):
    return lambda plane: left[i, plane, :] * right[j, plane, :]


def own_products(refs):
    (own,) = refs
    return [product(own, 0, own, 0), product(own, 0, own, 1), product(own, 1, own, 1)]


def cross_products(refs):
    own, other = refs
    return [product(own, b, other, j) for b in range(2) for j in range(2)]


def mask_body(me_ref, device_ref, mask_ref, *out_refs):
    for turn_, out_ref in enumerate(out_refs):
        row = device_ref[me_ref[0] * 16 + turn_]
        out_ref[...] = mask_ref[pl.ds(row, NG, stride=SLAB), :]


def params():
    return pltpu.CompilerParams(vmem_limit_bytes=VMEM_LIMIT)


def cost(flops, moved):
    return pl.CostEstimate(flops=flops, bytes_accessed=moved, transcendentals=0)


def call(body, shape, args, fields, name):
    return pl.pallas_call(
        body,
        out_shape=jax.ShapeDtypeStruct(shape, jnp.float32),
        in_specs=[pl.BlockSpec(memory_space=pltpu.VMEM) for _ in args],
        out_specs=pl.BlockSpec(memory_space=pltpu.VMEM),
        scratch_shapes=[pltpu.VMEM((ROWS_ALL, NG), jnp.float32) for _ in range(fields)],
        compiler_params=params(),
        cost_estimate=cost(5 * 10**9, 4 * 10**6),
        name=name,
    )(*args)


def ahead(count, products_of, grids, name):
    tables = (pair(y_table()), pair(z_ahead()), shared_width())
    args = [*grids, *(jnp.asarray(table) for table in tables)]
    body = functools.partial(ahead_body, count, products_of, len(grids))
    return call(body, (2 * NG, layout(count)[1]), args, count, name)


def back(body, count, grids, values, name):
    tables = (pair(y_table().T), pair(z_back()), shared_width())
    args = [*grids, values, *(jnp.asarray(table) for table in tables)]
    return call(body, (2, SLAB * NG, NG), args, count, name)


def indexed(body, shapes, args, me, flops, name):
    vmem = lambda: pl.BlockSpec(memory_space=pltpu.VMEM)
    return pl.pallas_call(
        body,
        out_shape=shapes,
        grid_spec=pltpu.PrefetchScalarGridSpec(
            num_scalar_prefetch=2,
            grid=(),
            in_specs=[vmem() for _ in args],
            out_specs=[vmem() for _ in shapes],
        ),
        compiler_params=params(),
        cost_estimate=cost(flops, 2 * 10**6),
        name=name,
    )(me, jnp.asarray(device_table()), *args)


def middle(count, values, masks, me, name):
    args = [values, jnp.asarray(lane_rows(count)), jnp.asarray(pair(x_tables())), *masks]
    shape = jax.ShapeDtypeStruct(values.shape, jnp.float32)
    return indexed(middle_body, [shape], args, me, 2 * 10**9, name)[0]


def mask_rows(mask, me):
    shapes = [jax.ShapeDtypeStruct((NG, NG), jnp.int32)] * SLAB
    return indexed(mask_body, shapes, [mask.reshape(NG * SLAB, NG)], me, 10**6, "mask_rows")


def swap(values):
    size = values.shape[1]
    blocks = values.reshape(N_FFT, BLOCK, size)
    blocks = lax.all_to_all(blocks, "fft", split_axis=0, concat_axis=0, tiled=True)
    return blocks.reshape(2 * NG, size)


def body(orbitals, mask):
    me = lax.axis_index("fft").astype(jnp.int32)[None]
    count = lax.axis_size("band")
    other = lax.ppermute(orbitals, "band", [(i, (i + 1) % count) for i in range(count)])
    own = orbitals.reshape(2, SLAB * NG, NG)
    other = other.reshape(2, SLAB * NG, NG)

    sent_own = ahead(3, own_products, (own,), "ahead_own")
    sent_own, mask = lax.optimization_barrier((sent_own, mask))
    lines_own = swap(sent_own)
    masks = [
        lax.ppermute(rows, "fft", pairs)
        for rows, (pairs, _, _) in zip(mask_rows(mask, me), mask_rounds())
    ]
    other, masks = lax.optimization_barrier((other, masks))
    lines_cross = swap(ahead(4, cross_products, (own, other), "ahead_cross"))
    lines_own = swap(middle(3, lines_own, masks, me, "middle_own"))
    lines_cross = swap(middle(4, lines_cross, masks, me, "middle_cross"))
    total = back(back_own_body, 3, (own,), lines_own, "back_own")
    total = back(back_cross_body, 4, (other, total), lines_cross, "back_cross")
    return total.reshape(orbitals.shape)


def solution(mesh):
    in_specs = (P("band", "fft", None, None), P(None, "fft", None))
    out_specs = P("band", "fft", None, None)
    return jax.shard_map(body, mesh=mesh, in_specs=in_specs, out_specs=out_specs, check_vma=False)
```

profile of v0, /device:TPU:70, one launch (start us, length us, event | category | flops | bytes accessed | tf_op | source)
XLA Modules:
  0.0 154.5 jit_solution(4933626877375707167)
XLA Ops:
  0.0 1.0 copy-done.2
  1.0 1.0 copy-done.6
  2.1 0.9 copy-done.8
  3.0 0.9 copy-done.11
  3.9 2.9 %ahead_own.1 = f32[256,640]{1,0:T(8,128)} custom-call(f32[2,512,128]{2,1,0:T(8,128)S(1)} %bitcast.18, bf16[2,256,128]{2,1,0:T(8,128)(2,1)S(1)} %copy-done.11, bf16[2,512,256]{2,1,0:T(8,128)(2,1)S(1)} %copy-done.6, s32[256,128]{1,0:T(8,128)S(1)} %copy-done.8), custom_call_target="tpu_custom_call" | custom-call | flops 5000000000 | bytes 4000000 | tf_op jit(solution)/shard_map/ahead_own/pallas_call | solution.py:422
  6.8 13.3 %all-to-all-start = ((f32[32,8,640]{2,1,0:T(8,128)}), f32[32,8,640]{2,1,0:T(8,128)S(1)}, u32[]{:S(2)}, u32[]{:S(2)}) async-start(f32[32,8,640]{2,1,0:T(8,128)} %bitcast.4), calls=%async_computation | async-start | bytes 1310720 | tf_op jit(solution)/shard_map/all_to_all | solution.py:478
  20.1 1.9 %collective-permute-start = (f32[2,4,128,128]{3,2,1,0:T(8,128)S(1)}, f32[2,4,128,128]{3,2,1,0:T(8,128)S(1)}, u32[]{:S(2)}, u32[]{:S(2)}) collective-permute-start(f32[2,4,128,128]{3,2,1,0:T(8,128)S(1)} %copy-done.3), channel_id=1, source_target_pairs={{0,32},{32,64},{64,96},{96,128},{128,160},{160,192},{192,224},{224... | collective-permute-start | bytes 1572872 | tf_op jit(solution)/shard_map/ppermute | solution.py:485
  22.1 0.0 copy-start.1
  22.1 0.7 copy-done.1
  22.8 0.6 mask_rows.1
  23.4 7.3 %collective-permute-start.1 = (s32[128,128]{1,0:T(8,128)S(1)}, s32[128,128]{1,0:T(8,128)S(1)}, u32[]{:S(2)}, u32[]{:S(2)}) collective-permute-start(s32[128,128]{1,0:T(8,128)S(1)} %get-tuple-element.17), channel_id=1, source_target_pairs={{0,3},{1,13},{2,21},{3,29},{4,31},{5,11},{6,19},{7,27},{8,5},{9,9}... | collective-permute-start | bytes 196616 | tf_op jit(solution)/shard_map/ppermute | solution.py:493
  30.7 2.2 %collective-permute-start.2 = (s32[128,128]{1,0:T(8,128)S(1)}, s32[128,128]{1,0:T(8,128)S(1)}, u32[]{:S(2)}, u32[]{:S(2)}) collective-permute-start(s32[128,128]{1,0:T(8,128)S(1)} %get-tuple-element.18), channel_id=1, source_target_pairs={{0,1},{1,11},{2,19},{3,27},{4,5},{5,7},{6,15},{7,23},{8,31},{9,13}... | collective-permute-start | bytes 196616 | tf_op jit(solution)/shard_map/ppermute | solution.py:493
  32.9 4.6 %collective-permute-start.3 = (s32[128,128]{1,0:T(8,128)S(1)}, s32[128,128]{1,0:T(8,128)S(1)}, u32[]{:S(2)}, u32[]{:S(2)}) collective-permute-start(s32[128,128]{1,0:T(8,128)S(1)} %get-tuple-element.19), channel_id=1, source_target_pairs={{0,5},{1,9},{2,17},{3,25},{4,3},{5,13},{6,21},{7,29},{8,1},{9,7},{... | collective-permute-start | bytes 196616 | tf_op jit(solution)/shard_map/ppermute | solution.py:493
  37.5 4.3 %collective-permute-start.4 = (s32[128,128]{1,0:T(8,128)S(1)}, s32[128,128]{1,0:T(8,128)S(1)}, u32[]{:S(2)}, u32[]{:S(2)}) collective-permute-start(s32[128,128]{1,0:T(8,128)S(1)} %get-tuple-element.20), channel_id=1, source_target_pairs={{0,0},{1,7},{2,15},{3,23},{4,1},{5,9},{6,17},{7,25},{8,3},{9,11},{... | collective-permute-start | bytes 196616 | tf_op jit(solution)/shard_map/ppermute | solution.py:493
  41.8 10.4 %collective-permute-done.1.rest_0_ = s32[128,128]{1,0:T(8,128)S(1)} collective-permute-done((s32[128,128]{1,0:T(8,128)S(1)}, s32[128,128]{1,0:T(8,128)S(1)}, u32[]{:S(2)}, u32[]{:S(2)}) %collective-permute-start.1) | collective-permute-done | bytes 65568 | tf_op jit(solution)/shard_map/ppermute | solution.py:493
  52.2 3.3 %ahead_cross.1 = f32[256,896]{1,0:T(8,128)} custom-call(f32[2,512,128]{2,1,0:T(8,128)S(1)} %bitcast.19, f32[2,512,128]{2,1,0:T(8,128)S(1)} %bitcast.21, bf16[2,256,128]{2,1,0:T(8,128)(2,1)S(1)} %copy-done.12, bf16[2,512,256]{2,1,0:T(8,128)(2,1)S(1)} %copy-done.7, s32[256,128]{1,0:T(8,128)S(1)} %copy-done.9), custom_call_target="tpu_custom_call" | custom-call | flops 5000000000 | bytes 4000000 | tf_op jit(solution)/shard_map/ahead_cross/pallas_call | solution.py:422
  55.6 14.6 %all-to-all-start.2 = ((f32[32,8,896]{2,1,0:T(8,128)}), f32[32,8,896]{2,1,0:T(8,128)S(1)}, u32[]{:S(2)}, u32[]{:S(2)}) async-start(f32[32,8,896]{2,1,0:T(8,128)} %bitcast.8), calls=%async_computation.2 | async-start | bytes 1835008 | tf_op jit(solution)/shard_map/all_to_all | solution.py:478
  70.2 0.0 copy-start.14
  70.2 0.7 copy-done.14
  70.9 3.1 %middle_own.1 = f32[256,640]{1,0:T(8,128)} custom-call(s32[1]{0:T(128)} %bitcast.1.me_ref, s32[512]{0:T(512)S(1)} %copy-done.1, f32[256,640]{1,0:T(8,128)S(1)} %bitcast.15, s32[8,640]{1,0:T(8,128)S(1)} %copy-done.14, bf16[2,512,256]{2,1,0:T(8,128)(2,1)S(1)} %copy-done.5, s32[128,128]{1,0:T(8,128)S(1)} %collective-permute-done.1.rest_0_, ...), custom_call_target="tpu_custom_call" | custom-call | flops 2000000000 | bytes 2000000 | tf_op jit(solution)/shard_map/middle_own/pallas_call | solution.py:449
  74.0 20.9 %all-to-all-done.2 = f32[32,8,896]{2,1,0:T(8,128)S(1)} async-done(((f32[32,8,896]{2,1,0:T(8,128)}), f32[32,8,896]{2,1,0:T(8,128)S(1)}, u32[]{:S(2)}, u32[]{:S(2)}) %all-to-all-start.2) | async-done | bytes 917536 | tf_op jit(solution)/shard_map/all_to_all | solution.py:478
  95.0 5.2 %all-to-all-start.1 = ((f32[32,8,640]{2,1,0:T(8,128)}), f32[32,8,640]{2,1,0:T(8,128)S(1)}, u32[]{:S(2)}, u32[]{:S(2)}) async-start(f32[32,8,640]{2,1,0:T(8,128)} %bitcast.6), calls=%async_computation.1 | async-start | bytes 1310720 | tf_op jit(solution)/shard_map/all_to_all | solution.py:478
  100.2 0.0 copy-start.13
  100.2 0.7 copy-done.13
  101.0 3.7 %middle_cross.1 = f32[256,896]{1,0:T(8,128)} custom-call(s32[1]{0:T(128)} %bitcast.1.me_ref, s32[512]{0:T(512)S(1)} %copy-done.1, f32[256,896]{1,0:T(8,128)S(1)} %bitcast.13, s32[8,896]{1,0:T(8,128)S(1)} %copy-done.13, bf16[2,512,256]{2,1,0:T(8,128)(2,1)S(1)} %copy-done.5, s32[128,128]{1,0:T(8,128)S(1)} %collective-permute-done.1.rest_0_, ...), custom_call_target="tpu_custom_call" | custom-call | flops 2000000000 | bytes 2000000 | tf_op jit(solution)/shard_map/middle_cross/pallas_call | solution.py:449
  104.6 15.6 %all-to-all-done.1 = f32[32,8,640]{2,1,0:T(8,128)S(1)} async-done(((f32[32,8,640]{2,1,0:T(8,128)}), f32[32,8,640]{2,1,0:T(8,128)S(1)}, u32[]{:S(2)}, u32[]{:S(2)}) %all-to-all-start.1) | async-done | bytes 655392 | tf_op jit(solution)/shard_map/all_to_all | solution.py:478
  120.2 5.0 %all-to-all-start.3 = ((f32[32,8,896]{2,1,0:T(8,128)}), f32[32,8,896]{2,1,0:T(8,128)S(1)}, u32[]{:S(2)}, u32[]{:S(2)}) async-start(f32[32,8,896]{2,1,0:T(8,128)} %bitcast.10), calls=%async_computation.3 | async-start | bytes 1835008 | tf_op jit(solution)/shard_map/all_to_all | solution.py:478
  125.2 1.7 %back_own.1.sum_ref = f32[2,512,128]{2,1,0:T(8,128)S(1)} custom-call(f32[2,512,128]{2,1,0:T(8,128)S(1)} %bitcast.20, f32[256,640]{1,0:T(8,128)S(1)} %bitcast.16, bf16[2,128,256]{2,1,0:T(8,128)(2,1)S(1)} %copy-done.10, bf16[2,512,256]{2,1,0:T(8,128)(2,1)S(1)} %copy-done.4, s32[256,128]{1,0:T(8,128)S(1)} %copy-done.9), custom_call_target="tpu_custom_call" | custom-call | flops 5000000000 | bytes 4000000 | tf_op jit(solution)/shard_map/back_own/pallas_call | solution.py:422
  127.0 0.8 copy-done.15
  127.7 23.1 %all-to-all-done.3 = f32[32,8,896]{2,1,0:T(8,128)S(1)} async-done(((f32[32,8,896]{2,1,0:T(8,128)}), f32[32,8,896]{2,1,0:T(8,128)S(1)}, u32[]{:S(2)}, u32[]{:S(2)}) %all-to-all-start.3) | async-done | bytes 917536 | tf_op jit(solution)/shard_map/all_to_all | solution.py:478
  150.8 1.0 copy-done.16
  151.9 2.7 %back_cross.1 = f32[2,512,128]{2,1,0:T(8,128)} custom-call(f32[2,512,128]{2,1,0:T(8,128)S(1)} %bitcast.22, f32[2,512,128]{2,1,0:T(8,128)S(1)} %copy-done.16, f32[256,896]{1,0:T(8,128)S(1)} %bitcast.14, bf16[2,128,256]{2,1,0:T(8,128)(2,1)S(1)} %copy-done.10, bf16[2,512,256]{2,1,0:T(8,128)(2,1)S(1)} %copy-done.4, s32[256,128]{1,0:T(8,128)S(1)} %copy-done.9), custom_call_target="tpu_custom_call" | custom-call | flops 5000000000 | bytes 4000000 | tf_op jit(solution)/shard_map/back_cross/pallas_call | solution.py:422
  (27 shorter events, 0.1 us)
Async XLA Ops:
  0.0 1.0 copy-start.2
  1.0 1.0 copy-start.6
  2.1 0.9 copy-start.8
  3.0 0.9 copy-start.11
  6.8 13.3 %copy-start.3 = (f32[2,4,128,128]{3,2,1,0:T(8,128)S(1)}, f32[2,4,128,128]{3,2,1,0:T(8,128)}, u32[]{:S(2)}) copy-start(f32[2,4,128,128]{3,2,1,0:T(8,128)} %param.16) | copy-start | bytes 1572868
  6.8 15.3 %copy-start = (s32[128,4,128]{2,1,0:T(4,128)S(1)}, s32[128,4,128]{2,1,0:T(4,128)}, u32[]{:S(2)}) copy-start(s32[128,4,128]{2,1,0:T(4,128)} %param.17) | copy-start | bytes 786436
  6.8 45.3 %copy-start.7 = (bf16[2,512,256]{2,1,0:T(8,128)(2,1)S(1)}, bf16[2,512,256]{2,1,0:T(8,128)(2,1)}, u32[]{:S(2)}) copy-start(bf16[2,512,256]{2,1,0:T(8,128)(2,1)} %constant.23.clone.refs_2_.refs_3_) | copy-start | bytes 1572868
  6.8 48.7 %all-to-all-start = ((f32[32,8,640]{2,1,0:T(8,128)}), f32[32,8,640]{2,1,0:T(8,128)S(1)}, u32[]{:S(2)}, u32[]{:S(2)}) async-start(f32[32,8,640]{2,1,0:T(8,128)} %bitcast.4), calls=%async_computation | async-start | bytes 1310720 | tf_op jit(solution)/shard_map/all_to_all | solution.py:478
  20.1 32.0 %collective-permute-start = (f32[2,4,128,128]{3,2,1,0:T(8,128)S(1)}, f32[2,4,128,128]{3,2,1,0:T(8,128)S(1)}, u32[]{:S(2)}, u32[]{:S(2)}) collective-permute-start(f32[2,4,128,128]{3,2,1,0:T(8,128)S(1)} %copy-done.3), channel_id=1, source_target_pairs={{0,32},{32,64},{64,96},{96,128},{128,160},{160,192},{192,224},{224... | collective-permute-start | bytes 1572872 | tf_op jit(solution)/shard_map/ppermute | solution.py:485
  22.1 0.7 copy-start.1
  22.8 29.4 %copy-start.9 = (s32[256,128]{1,0:T(8,128)S(1)}, s32[256,128]{1,0:T(8,128)}, u32[]{:S(2)}) copy-start(s32[256,128]{1,0:T(8,128)} %constant.24.clone.refs_3_.width_ref.refs_4_) | copy-start | bytes 393220
  22.8 29.4 %copy-start.12 = (bf16[2,256,128]{2,1,0:T(8,128)(2,1)S(1)}, bf16[2,256,128]{2,1,0:T(8,128)(2,1)}, u32[]{:S(2)}) copy-start(bf16[2,256,128]{2,1,0:T(8,128)(2,1)} %constant.22.clone.refs_1_.refs_2_) | copy-start | bytes 393220
  23.4 28.8 %collective-permute-start.1 = (s32[128,128]{1,0:T(8,128)S(1)}, s32[128,128]{1,0:T(8,128)S(1)}, u32[]{:S(2)}, u32[]{:S(2)}) collective-permute-start(s32[128,128]{1,0:T(8,128)S(1)} %get-tuple-element.17), channel_id=1, source_target_pairs={{0,3},{1,13},{2,21},{3,29},{4,31},{5,11},{6,19},{7,27},{8,5},{9,9}... | collective-permute-start | bytes 196616 | tf_op jit(solution)/shard_map/ppermute | solution.py:493
  30.7 21.5 %collective-permute-start.2 = (s32[128,128]{1,0:T(8,128)S(1)}, s32[128,128]{1,0:T(8,128)S(1)}, u32[]{:S(2)}, u32[]{:S(2)}) collective-permute-start(s32[128,128]{1,0:T(8,128)S(1)} %get-tuple-element.18), channel_id=1, source_target_pairs={{0,1},{1,11},{2,19},{3,27},{4,5},{5,7},{6,15},{7,23},{8,31},{9,13}... | collective-permute-start | bytes 196616 | tf_op jit(solution)/shard_map/ppermute | solution.py:493
  32.9 19.3 %collective-permute-start.3 = (s32[128,128]{1,0:T(8,128)S(1)}, s32[128,128]{1,0:T(8,128)S(1)}, u32[]{:S(2)}, u32[]{:S(2)}) collective-permute-start(s32[128,128]{1,0:T(8,128)S(1)} %get-tuple-element.19), channel_id=1, source_target_pairs={{0,5},{1,9},{2,17},{3,25},{4,3},{5,13},{6,21},{7,29},{8,1},{9,7},{... | collective-permute-start | bytes 196616 | tf_op jit(solution)/shard_map/ppermute | solution.py:493
  37.5 14.7 %collective-permute-start.4 = (s32[128,128]{1,0:T(8,128)S(1)}, s32[128,128]{1,0:T(8,128)S(1)}, u32[]{:S(2)}, u32[]{:S(2)}) collective-permute-start(s32[128,128]{1,0:T(8,128)S(1)} %get-tuple-element.20), channel_id=1, source_target_pairs={{0,0},{1,7},{2,15},{3,23},{4,1},{5,9},{6,17},{7,25},{8,3},{9,11},{... | collective-permute-start | bytes 196616 | tf_op jit(solution)/shard_map/ppermute | solution.py:493
  55.5 14.6 %copy-start.5 = (bf16[2,512,256]{2,1,0:T(8,128)(2,1)S(1)}, bf16[2,512,256]{2,1,0:T(8,128)(2,1)}, u32[]{:S(2)}) copy-start(bf16[2,512,256]{2,1,0:T(8,128)(2,1)} %constant.27.clone.table_ref) | copy-start | bytes 1572868
  55.6 39.4 %all-to-all-start.2 = ((f32[32,8,896]{2,1,0:T(8,128)}), f32[32,8,896]{2,1,0:T(8,128)S(1)}, u32[]{:S(2)}, u32[]{:S(2)}) async-start(f32[32,8,896]{2,1,0:T(8,128)} %bitcast.8), calls=%async_computation.2 | async-start | bytes 1835008 | tf_op jit(solution)/shard_map/all_to_all | solution.py:478
  70.2 0.7 copy-start.14
  95.0 25.3 %all-to-all-start.1 = ((f32[32,8,640]{2,1,0:T(8,128)}), f32[32,8,640]{2,1,0:T(8,128)S(1)}, u32[]{:S(2)}, u32[]{:S(2)}) async-start(f32[32,8,640]{2,1,0:T(8,128)} %bitcast.6), calls=%async_computation.1 | async-start | bytes 1310720 | tf_op jit(solution)/shard_map/all_to_all | solution.py:478
  100.2 0.8 copy-start.13
  120.2 5.0 %copy-start.4 = (bf16[2,512,256]{2,1,0:T(8,128)(2,1)S(1)}, bf16[2,512,256]{2,1,0:T(8,128)(2,1)}, u32[]{:S(2)}) copy-start(bf16[2,512,256]{2,1,0:T(8,128)(2,1)} %constant.30.clone.z_ref) | copy-start | bytes 1572868
  120.2 5.0 %copy-start.10 = (bf16[2,128,256]{2,1,0:T(8,128)(2,1)S(1)}, bf16[2,128,256]{2,1,0:T(8,128)(2,1)}, u32[]{:S(2)}) copy-start(bf16[2,128,256]{2,1,0:T(8,128)(2,1)} %constant.29.clone.y_ref) | copy-start | bytes 393220
  120.2 30.6 %all-to-all-start.3 = ((f32[32,8,896]{2,1,0:T(8,128)}), f32[32,8,896]{2,1,0:T(8,128)S(1)}, u32[]{:S(2)}, u32[]{:S(2)}) async-start(f32[32,8,896]{2,1,0:T(8,128)} %bitcast.10), calls=%async_computation.3 | async-start | bytes 1835008 | tf_op jit(solution)/shard_map/all_to_all | solution.py:478
  126.9 0.8 copy-start.15
  150.8 1.0 copy-start.16
where the time goes:
time: 155 us
  waiting for transfers between devices  70 us (45%)
  starting transfers between devices  58.4 us (38%)
  Pallas kernels  18 us (12%)
  local copies, waits for them, and re-layouts  7.88 us (5%)
    all_to_all x4, waiting for transfers between devices, swap(): lax.all_to_all(blocks, 'fft', split_axis=0, concat_axis=0, tiled=True)  59.6 us
    all_to_all x4, starting transfers between devices, swap(): lax.all_to_all(blocks, 'fft', split_axis=0, concat_axis=0, tiled=True)  38.1 us
    ppermute x4, starting transfers between devices, body(): lax.ppermute(rows, 'fft', pairs)  18.4 us
    pallas_call x4, Pallas kernels, call(): pl.pallas_call(body, out_shape=jax.ShapeDtypeStruct(shape, jnp.float32),...  10.7 us
    ppermute x4, waiting for transfers between devices, body(): lax.ppermute(rows, 'fft', pairs)  10.4 us
    unnamed x34, local copies, waits for them, and re-layouts  7.88 us
    pallas_call x3, Pallas kernels, indexed(): pl.pallas_call(body, out_shape=shapes, grid_spec=pltpu.PrefetchScalarGrid...  7.36 us
  transfers between devices with their start and end apart: 9, of which 4 were waited for; matrix products, arithmetic and copies ran while one was open for 0% of the time, Pallas kernels for 8%

commit v1 on v0

--- a/solution.py
+++ b/solution.py
@@ -19,6 +19,7 @@
 ROWS_ALL = 4 * 2 * NG
 NO_LINE = 999
 VMEM_LIMIT = 20 * 1024 * 1024
+VMEM_MOST = 56 * 1024 * 1024
 
 
 def kept(ky):
@@ -281,11 +282,21 @@
 
 
 def middle_body(me_ref, device_ref, x_ref, lane_ref, table_ref, *rest):
-    *mask_refs, out_ref = rest
+    *mask_refs, out_ref, done = rest
     size = x_ref.shape[1]
+    before = out_ref.shape[1] - size
+    if before:
+        ready_ref, *mask_refs = mask_refs
+        copy = pltpu.make_async_copy(ready_ref, out_ref.at[:, :before], done)
+        copy.start()
     base = me_ref[0] * 16
-    masks = [ref[...].astype(jnp.float32).astype(jnp.bfloat16) for ref in mask_refs]
-    zero_mask = mask_refs[ZERO_ROUND][0:1, HALF : HALF + 1].astype(jnp.float32)
+    spot = (iota((HALF, LANES), 0) == 0) & (iota((HALF, LANES), 1) == HALF - 1)
+    masks = []
+    for ref in mask_refs:
+        cells = ref[...].astype(jnp.float32)
+        high = jnp.where(spot, 0.0, pltpu.roll(cells, HALF, 1))
+        masks.append(jnp.concatenate([cells, high], axis=0).astype(jnp.bfloat16))
+    zero_mask = mask_refs[ZERO_ROUND][0:1, LANES - 1 : LANES].astype(jnp.float32)
     is_imag = iota((2 * NG, LANES), 0) % BLOCK >= SLAB
     kx = iota((NG, LANES), 0)
     signed = jnp.where(kx < HALF, kx, kx - NG)
@@ -319,11 +330,14 @@
         spectrum = dot3(forward, split(beside(values)))
         weight = jnp.concatenate([beside(real), beside(imag)], axis=0)
         width = LANES * len(values)
-        out_ref[:, step : step + width] = dot3(inverse, split(spectrum * weight))
-
-
-def potentials(count, lines_ref, y_ref, z_ref, width_ref, grids):
+        out_ref[:, before + step : before + step + width] = dot3(inverse, split(spectrum * weight))
+    if before:
+        copy.wait()
+
+
+def potentials(count, offset, lines_ref, y_ref, z_ref, width_ref, grids):
     pieces, _ = layout(count)
+    pieces = [(*piece[:4], piece[4] + offset) for piece in pieces]
     lane = iota((2 * NG, LANES), 1)
     is_imag = iota((2 * NG, LANES), 0) % BLOCK >= SLAB
     sides = {}
@@ -370,24 +384,20 @@
     return plane_of
 
 
-def back_own_body(own_ref, lines_ref, y_ref, z_ref, width_ref, out_ref, *grids):
-    plane_of = potentials(3, lines_ref, y_ref, z_ref, width_ref, grids)
+def back_body(own_ref, other_ref, lines_ref, y_ref, z_ref, width_ref, out_ref, *grids):
+    tables = (lines_ref, y_ref, z_ref, width_ref)
+    own_plane = potentials(3, 0, *tables, grids[:3])
+    cross_plane = potentials(4, layout(3)[1], *tables, grids[3:])
     for x in range(SLAB):
         plane = slice(NG * x, NG * x + NG)
-        first, mixed, second = plane_of(x)
-        out_ref[0, plane, :] = first * own_ref[0, plane, :] + mixed * own_ref[1, plane, :]
-        out_ref[1, plane, :] = mixed * own_ref[0, plane, :] + second * own_ref[1, plane, :]
-
-
-def back_cross_body(other_ref, sum_ref, lines_ref, y_ref, z_ref, width_ref, out_ref, *grids):
-    plane_of = potentials(4, lines_ref, y_ref, z_ref, width_ref, grids)
-    for x in range(SLAB):
-        plane = slice(NG * x, NG * x + NG)
-        cells = plane_of(x)
-        for band in range(2):
-            total = cells[2 * band] * other_ref[0, plane, :]
-            total += cells[2 * band + 1] * other_ref[1, plane, :]
-            out_ref[band, plane, :] = -0.5 * (sum_ref[band, plane, :] + total)
+        own = [own_ref[band, plane, :] for band in range(2)]
+        other = [other_ref[band, plane, :] for band in range(2)]
+        first, mixed, second = own_plane(x)
+        cross = cross_plane(x)
+        total = first * own[0] + mixed * own[1] + (cross[0] * other[0] + cross[1] * other[1])
+        out_ref[0, plane, :] = -0.5 * total
+        total = mixed * own[0] + second * own[1] + (cross[2] * other[0] + cross[3] * other[1])
+        out_ref[1, plane, :] = -0.5 * total
 
 
 def product(left, i, right, j):
@@ -405,46 +415,51 @@
 
 
 def mask_body(me_ref, device_ref, mask_ref, *out_refs):
+    lane = iota((HALF, LANES), 1)
     for turn_, out_ref in enumerate(out_refs):
         row = device_ref[me_ref[0] * 16 + turn_]
-        out_ref[...] = mask_ref[pl.ds(row, NG, stride=SLAB), :]
-
-
-def params():
-    return pltpu.CompilerParams(vmem_limit_bytes=VMEM_LIMIT)
+        low = mask_ref[pl.ds(row, HALF, stride=SLAB), :]
+        high = mask_ref[pl.ds(row + HALF * SLAB, HALF, stride=SLAB), :]
+        packed = jnp.where(lane < HALF, low, pltpu.roll(high, HALF, 1))
+        spot = (iota((HALF, LANES), 0) == 0) & (lane == LANES - 1)
+        out_ref[...] = jnp.where(spot, low[0:1, HALF : HALF + 1], packed)
+
+
+def params(limit=VMEM_LIMIT):
+    return pltpu.CompilerParams(vmem_limit_bytes=limit)
 
 
 def cost(flops, moved):
     return pl.CostEstimate(flops=flops, bytes_accessed=moved, transcendentals=0)
 
 
-def call(body, shape, args, fields, name):
+def call(body, shape, args, fields, flops, limit, name):
     return pl.pallas_call(
         body,
         out_shape=jax.ShapeDtypeStruct(shape, jnp.float32),
         in_specs=[pl.BlockSpec(memory_space=pltpu.VMEM) for _ in args],
         out_specs=pl.BlockSpec(memory_space=pltpu.VMEM),
         scratch_shapes=[pltpu.VMEM((ROWS_ALL, NG), jnp.float32) for _ in range(fields)],
-        compiler_params=params(),
-        cost_estimate=cost(5 * 10**9, 4 * 10**6),
+        compiler_params=params(limit),
+        cost_estimate=cost(flops, 4 * 10**6),
         name=name,
     )(*args)
 
 
-def ahead(count, products_of, grids, name):
+def ahead(count, products_of, grids, flops, limit, name):
     tables = (pair(y_table()), pair(z_ahead()), shared_width())
     args = [*grids, *(jnp.asarray(table) for table in tables)]
     body = functools.partial(ahead_body, count, products_of, len(grids))
-    return call(body, (2 * NG, layout(count)[1]), args, count, name)
-
-
-def back(body, count, grids, values, name):
+    return call(body, (2 * NG, layout(count)[1]), args, count, flops, limit, name)
+
+
+def back(own, other, values):
     tables = (pair(y_table().T), pair(z_back()), shared_width())
-    args = [*grids, values, *(jnp.asarray(table) for table in tables)]
-    return call(body, (2, SLAB * NG, NG), args, count, name)
-
-
-def indexed(body, shapes, args, me, flops, name):
+    args = [own, other, values, *(jnp.asarray(table) for table in tables)]
+    return call(back_body, (2, SLAB * NG, NG), args, 7, 5 * 10**9, VMEM_LIMIT, "back")
+
+
+def indexed(body, shapes, args, me, flops, name, scratch=(), away=()):
     vmem = lambda: pl.BlockSpec(memory_space=pltpu.VMEM)
     return pl.pallas_call(
         body,
@@ -452,8 +467,12 @@
         grid_spec=pltpu.PrefetchScalarGridSpec(
             num_scalar_prefetch=2,
             grid=(),
-            in_specs=[vmem() for _ in args],
+            in_specs=[
+                pl.BlockSpec(memory_space=pl.ANY) if spot in away else vmem()
+                for spot in range(len(args))
+            ],
             out_specs=[vmem() for _ in shapes],
+            scratch_shapes=list(scratch),
         ),
         compiler_params=params(),
         cost_estimate=cost(flops, 2 * 10**6),
@@ -461,14 +480,16 @@
     )(me, jnp.asarray(device_table()), *args)
 
 
-def middle(count, values, masks, me, name):
-    args = [values, jnp.asarray(lane_rows(count)), jnp.asarray(pair(x_tables())), *masks]
-    shape = jax.ShapeDtypeStruct(values.shape, jnp.float32)
-    return indexed(middle_body, [shape], args, me, 2 * 10**9, name)[0]
+def middle(count, values, ready, masks, me, name):
+    args = [values, jnp.asarray(lane_rows(count)), jnp.asarray(pair(x_tables())), *ready, *masks]
+    size = values.shape[1] + sum(part.shape[1] for part in ready)
+    shape = jax.ShapeDtypeStruct((2 * NG, size), jnp.float32)
+    scratch, away = [pltpu.SemaphoreType.DMA], [3] if ready else []
+    return indexed(middle_body, [shape], args, me, 2 * 10**9, name, scratch, away)[0]
 
 
 def mask_rows(mask, me):
-    shapes = [jax.ShapeDtypeStruct((NG, NG), jnp.int32)] * SLAB
+    shapes = [jax.ShapeDtypeStruct((HALF, NG), jnp.int32)] * SLAB
     return indexed(mask_body, shapes, [mask.reshape(NG * SLAB, NG)], me, 10**6, "mask_rows")
 
 
@@ -486,20 +507,19 @@
     own = orbitals.reshape(2, SLAB * NG, NG)
     other = other.reshape(2, SLAB * NG, NG)
 
-    sent_own = ahead(3, own_products, (own,), "ahead_own")
+    sent_own = ahead(3, own_products, (own,), 2 * 10**10, VMEM_MOST, "ahead_own")
     sent_own, mask = lax.optimization_barrier((sent_own, mask))
     lines_own = swap(sent_own)
     masks = [
         lax.ppermute(rows, "fft", pairs)
         for rows, (pairs, _, _) in zip(mask_rows(mask, me), mask_rounds())
     ]
-    other, masks = lax.optimization_barrier((other, masks))
-    lines_cross = swap(ahead(4, cross_products, (own, other), "ahead_cross"))
-    lines_own = swap(middle(3, lines_own, masks, me, "middle_own"))
-    lines_cross = swap(middle(4, lines_cross, masks, me, "middle_cross"))
-    total = back(back_own_body, 3, (own,), lines_own, "back_own")
-    total = back(back_cross_body, 4, (other, total), lines_cross, "back_cross")
-    return total.reshape(orbitals.shape)
+    sent_cross = ahead(4, cross_products, (own, other), 2 * 10**10, VMEM_LIMIT, "ahead_cross")
+    (sent_cross, masks[0], masks[1]) = lax.optimization_barrier((sent_cross, masks[0], masks[1]))
+    lines_cross = swap(sent_cross)
+    lines_own = middle(3, lines_own, [], masks, me, "middle_own")
+    lines = swap(middle(4, lines_cross, [lines_own], masks, me, "middle_cross"))
+    return back(own, other, lines).reshape(orbitals.shape)
 
 
 def solution(mesh):

time: 155 us -> 136 us (0.88)
  the two profiles are of different devices: /device:TPU:70 before, /device:TPU:2 now
where the time goes in v1:
time: 136 us
  blocking collectives  49.7 us (37%)
  starting transfers between devices  42.4 us (31%)
  waiting for transfers between devices  24.1 us (18%)
  Pallas kernels  17.5 us (13%)
  local copies, waits for them, and re-layouts  1.99 us (1%)
    all_to_all x1, blocking collectives, swap(): lax.all_to_all(blocks, 'fft', split_axis=0, concat_axis=0, tiled=True)  49.7 us
    all_to_all x2, starting transfers between devices, swap(): lax.all_to_all(blocks, 'fft', split_axis=0, concat_axis=0, tiled=True)  22.1 us
    ppermute x4, waiting for transfers between devices, body(): lax.ppermute(rows, 'fft', pairs)  21.2 us
    ppermute x4, starting transfers between devices, body(): lax.ppermute(rows, 'fft', pairs)  18.4 us
    pallas_call x3, Pallas kernels, call(): pl.pallas_call(body, out_shape=jax.ShapeDtypeStruct(shape, jnp.float32),...  11.8 us
    pallas_call x3, Pallas kernels, indexed(): pl.pallas_call(body, out_shape=shapes, grid_spec=pltpu.PrefetchScalarGrid...  5.74 us
    all_to_all x2, waiting for transfers between devices, swap(): lax.all_to_all(blocks, 'fft', split_axis=0, concat_axis=0, tiled=True)  2.88 us
  transfers between devices with their start and end apart: 7, of which 3 were waited for; matrix products, arithmetic and copies ran while one was open for 0% of the time, Pallas kernels for 8%

profile of v1, /device:TPU:2, one launch (start us, length us, event | category | flops | bytes accessed | tf_op | source)
XLA Modules:
  0.0 135.8 jit_solution(13723243680879866032)
XLA Ops:
  0.0 1.9 %collective-permute-start = (f32[2,4,128,128]{3,2,1,0:T(8,128)}, f32[2,4,128,128]{3,2,1,0:T(8,128)S(1)}, u32[]{:S(2)}, u32[]{:S(2)}) collective-permute-start(f32[2,4,128,128]{3,2,1,0:T(8,128)} %param.14), channel_id=1, source_target_pairs={{0,32},{32,64},{64,96},{96,128},{128,160},{160,192},{192,224},{224... | collective-permute-start | bytes 1572872 | tf_op jit(solution)/shard_map/ppermute | solution.py:506
  1.9 0.0 copy-start
  1.9 0.0 copy-start.1
  1.9 4.3 %ahead_own.1 = f32[256,640]{1,0:T(8,128)} custom-call(f32[2,512,128]{2,1,0:T(8,128)} %bitcast.16, bf16[2,256,128]{2,1,0:T(8,128)(2,1)} %constant.22.clone.refs_2_.refs_1_, bf16[2,512,256]{2,1,0:T(8,128)(2,1)} %constant.23.clone.refs_3_.refs_2_, s32[256,128]{1,0:T(8,128)} %constant.24.clone.refs_4_.refs_3_.width_ref), custom_call_target="tpu_custom_call" | custom-call | flops 20000000000 | bytes 4000000 | tf_op jit(solution)/shard_map/ahead_own/pallas_call | solution.py:437
  6.2 13.9 %all-to-all-start.1 = ((f32[32,8,640]{2,1,0:T(8,128)}), f32[32,8,640]{2,1,0:T(8,128)S(1)}, u32[]{:S(2)}, u32[]{:S(2)}) async-start(f32[32,8,640]{2,1,0:T(8,128)} %bitcast.21), calls=%async_computation.1 | async-start | bytes 1310720 | tf_op jit(solution)/shard_map/all_to_all | solution.py:499
  20.1 0.0 copy-done
  20.1 0.0 copy-done.1
  20.1 0.7 mask_rows.1
  20.8 5.5 %collective-permute-start.1 = (s32[64,128]{1,0:T(8,128)S(1)}, s32[64,128]{1,0:T(8,128)S(1)}, u32[]{:S(2)}, u32[]{:S(2)}) collective-permute-start(s32[64,128]{1,0:T(8,128)S(1)} %get-tuple-element.15), channel_id=1, source_target_pairs={{0,3},{1,13},{2,21},{3,29},{4,31},{5,11},{6,19},{7,27},{8,5},{9,9}... | collective-permute-start | bytes 98312 | tf_op jit(solution)/shard_map/ppermute | solution.py:514
  26.3 5.5 %collective-permute-start.2 = (s32[64,128]{1,0:T(8,128)S(1)}, s32[64,128]{1,0:T(8,128)S(1)}, u32[]{:S(2)}, u32[]{:S(2)}) collective-permute-start(s32[64,128]{1,0:T(8,128)S(1)} %get-tuple-element.16), channel_id=1, source_target_pairs={{0,1},{1,11},{2,19},{3,27},{4,5},{5,7},{6,15},{7,23},{8,31},{9,13}... | collective-permute-start | bytes 98312 | tf_op jit(solution)/shard_map/ppermute | solution.py:514
  31.8 0.0 collective-permute-done
  31.8 0.0 copy-done.2
  31.9 3.3 %ahead_cross.1 = f32[256,896]{1,0:T(8,128)} custom-call(f32[2,512,128]{2,1,0:T(8,128)S(1)} %bitcast.17, f32[2,512,128]{2,1,0:T(8,128)S(1)} %bitcast.19, bf16[2,256,128]{2,1,0:T(8,128)(2,1)S(1)} %copy-done.8, bf16[2,512,256]{2,1,0:T(8,128)(2,1)S(1)} %copy-done.5, s32[256,128]{1,0:T(8,128)S(1)} %copy-done.6), custom_call_target="tpu_custom_call" | custom-call | flops 20000000000 | bytes 4000000 | tf_op jit(solution)/shard_map/ahead_cross/pallas_call | solution.py:437
  35.2 4.6 %collective-permute-done.1.rest_0_.rest_1_ = s32[64,128]{1,0:T(8,128)S(1)} collective-permute-done((s32[64,128]{1,0:T(8,128)S(1)}, s32[64,128]{1,0:T(8,128)S(1)}, u32[]{:S(2)}, u32[]{:S(2)}) %collective-permute-start.1) | collective-permute-done | bytes 32800 | tf_op jit(solution)/shard_map/ppermute | solution.py:514
  39.8 0.0 collective-permute-done.2.rest_1_.rest_2_
  39.8 2.9 %all-to-all-done.1 = f32[32,8,640]{2,1,0:T(8,128)S(1)} async-done(((f32[32,8,640]{2,1,0:T(8,128)}), f32[32,8,640]{2,1,0:T(8,128)S(1)}, u32[]{:S(2)}, u32[]{:S(2)}) %all-to-all-start.1) | async-done | bytes 655392 | tf_op jit(solution)/shard_map/all_to_all | solution.py:499
  42.7 8.2 %all-to-all-start = ((f32[32,8,896]{2,1,0:T(8,128)}), f32[32,8,896]{2,1,0:T(8,128)S(1)}, u32[]{:S(2)}, u32[]{:S(2)}) async-start(f32[32,8,896]{2,1,0:T(8,128)} %bitcast.4), calls=%async_computation | async-start | bytes 1835008 | tf_op jit(solution)/shard_map/all_to_all | solution.py:499
  50.9 6.7 %collective-permute-start.3 = (s32[64,128]{1,0:T(8,128)S(1)}, s32[64,128]{1,0:T(8,128)S(1)}, u32[]{:S(2)}, u32[]{:S(2)}) collective-permute-start(s32[64,128]{1,0:T(8,128)S(1)} %get-tuple-element.21), channel_id=1, source_target_pairs={{0,5},{1,9},{2,17},{3,25},{4,3},{5,13},{6,21},{7,29},{8,1},{9,7},{... | collective-permute-start | bytes 98312 | tf_op jit(solution)/shard_map/ppermute | solution.py:514
  57.6 0.7 collective-permute-start.4
  58.3 16.6 %collective-permute-done.3.rest_2_.rest_3_ = s32[64,128]{1,0:T(8,128)S(1)} collective-permute-done((s32[64,128]{1,0:T(8,128)S(1)}, s32[64,128]{1,0:T(8,128)S(1)}, u32[]{:S(2)}, u32[]{:S(2)}) %collective-permute-start.3) | collective-permute-done | bytes 32800 | tf_op jit(solution)/shard_map/ppermute | solution.py:514
  74.9 0.0 collective-permute-done.4.rest_3_.rest_4_
  74.9 0.0 copy-done.10
  74.9 0.0 copy-start.9
  74.9 2.3 %middle_own.1.rest_0_ = f32[256,640]{1,0:T(8,128)S(1)} custom-call(s32[1]{0:T(128)} %bitcast.2.me_ref, s32[512]{0:T(512)S(1)} %copy-done.1, f32[256,640]{1,0:T(8,128)S(1)} %bitcast.14, s32[8,640]{1,0:T(8,128)S(1)} %copy-done.10, bf16[2,512,256]{2,1,0:T(8,128)(2,1)S(1)} %copy-done.4, s32[64,128]{1,0:T(8,128)S(1)} %collective-permute-done.1.rest_0_.rest_1_, ...), custom_call_target="tpu_custom_call" | custom-call | flops 2000000000 | bytes 2000000 | tf_op jit(solution)/shard_map/middle_own/pallas_call | solution.py:464
  77.2 0.8 copy-done.11
  78.0 0.0 all-to-all-done
  78.0 1.1 copy-done.12
  79.1 2.8 %middle_cross.1 = f32[256,1536]{1,0:T(8,128)S(1)} custom-call(s32[1]{0:T(128)} %bitcast.2.me_ref, s32[512]{0:T(512)S(1)} %copy-done.1, f32[256,896]{1,0:T(8,128)S(1)} %bitcast.13, s32[8,896]{1,0:T(8,128)S(1)} %copy-done.9, bf16[2,512,256]{2,1,0:T(8,128)(2,1)S(1)} %copy-done.4, f32[256,640]{1,0:T(8,128)S(1)} %copy-done.12, ...), custom_call_target="tpu_custom_call" | custom-call | flops 2000000000 | bytes 2000000 | tf_op jit(solution)/shard_map/middle_cross/pallas_call | solution.py:464
  81.9 0.0 copy-start.3
  81.9 0.0 copy-start.7
  81.9 49.7 %all_to_all.15 = f32[32,8,1536]{2,1,0:T(8,128)S(1)} all-to-all(f32[32,8,1536]{2,1,0:T(8,128)S(1)} %bitcast.11), channel_id=1, replica_groups=mesh['band'=16,'fft'=32] {'fft'}, dimensions={0} | all-to-all | bytes 3145728 | tf_op jit(solution)/shard_map/all_to_all | solution.py:499
  131.6 4.2 %back.1 = f32[2,512,128]{2,1,0:T(8,128)} custom-call(f32[2,512,128]{2,1,0:T(8,128)S(1)} %bitcast.18, f32[2,512,128]{2,1,0:T(8,128)S(1)} %bitcast.20, f32[256,1536]{1,0:T(8,128)S(1)} %bitcast.12, bf16[2,128,256]{2,1,0:T(8,128)(2,1)S(1)} %copy-done.7, bf16[2,512,256]{2,1,0:T(8,128)(2,1)S(1)} %copy-done.3, s32[256,128]{1,0:T(8,128)S(1)} %copy-done.6), custom_call_target="tpu_custom_call" | custom-call | flops 5000000000 | bytes 4000000 | tf_op jit(solution)/shard_map/back/pallas_call | solution.py:437
  (15 shorter events, 0.0 us)
Async XLA Ops:
  0.0 31.8 %collective-permute-start = (f32[2,4,128,128]{3,2,1,0:T(8,128)}, f32[2,4,128,128]{3,2,1,0:T(8,128)S(1)}, u32[]{:S(2)}, u32[]{:S(2)}) collective-permute-start(f32[2,4,128,128]{3,2,1,0:T(8,128)} %param.14), channel_id=1, source_target_pairs={{0,32},{32,64},{64,96},{96,128},{128,160},{160,192},{192,224},{224... | collective-permute-start | bytes 1572872 | tf_op jit(solution)/shard_map/ppermute | solution.py:506
  1.9 18.2 %copy-start = (s32[128,4,128]{2,1,0:T(4,128)S(1)}, s32[128,4,128]{2,1,0:T(4,128)}, u32[]{:S(2)}) copy-start(s32[128,4,128]{2,1,0:T(4,128)} %param.15) | copy-start | bytes 786436
  1.9 18.2 %copy-start.1 = (s32[512]{0:T(512)S(1)}, s32[512]{0:T(512)}, u32[]{:S(2)}) copy-start(s32[512]{0:T(512)} %constant.25.clone.device_ref) | copy-start | bytes 6148
  6.2 25.6 %copy-start.2 = (f32[2,4,128,128]{3,2,1,0:T(8,128)S(1)}, f32[2,4,128,128]{3,2,1,0:T(8,128)}, u32[]{:S(2)}) copy-start(f32[2,4,128,128]{3,2,1,0:T(8,128)} %param.14) | copy-start | bytes 1572868
  6.2 25.6 %copy-start.5 = (bf16[2,512,256]{2,1,0:T(8,128)(2,1)S(1)}, bf16[2,512,256]{2,1,0:T(8,128)(2,1)}, u32[]{:S(2)}) copy-start(bf16[2,512,256]{2,1,0:T(8,128)(2,1)} %constant.23.clone.refs_3_.refs_2_) | copy-start | bytes 1572868
  6.2 25.7 %copy-start.6 = (s32[256,128]{1,0:T(8,128)S(1)}, s32[256,128]{1,0:T(8,128)}, u32[]{:S(2)}) copy-start(s32[256,128]{1,0:T(8,128)} %constant.24.clone.refs_4_.refs_3_.width_ref) | copy-start | bytes 393220
  6.2 25.7 %copy-start.8 = (bf16[2,256,128]{2,1,0:T(8,128)(2,1)S(1)}, bf16[2,256,128]{2,1,0:T(8,128)(2,1)}, u32[]{:S(2)}) copy-start(bf16[2,256,128]{2,1,0:T(8,128)(2,1)} %constant.22.clone.refs_2_.refs_1_) | copy-start | bytes 393220
  6.2 36.5 %all-to-all-start.1 = ((f32[32,8,640]{2,1,0:T(8,128)}), f32[32,8,640]{2,1,0:T(8,128)S(1)}, u32[]{:S(2)}, u32[]{:S(2)}) async-start(f32[32,8,640]{2,1,0:T(8,128)} %bitcast.21), calls=%async_computation.1 | async-start | bytes 1310720 | tf_op jit(solution)/shard_map/all_to_all | solution.py:499
  20.8 19.0 %collective-permute-start.1 = (s32[64,128]{1,0:T(8,128)S(1)}, s32[64,128]{1,0:T(8,128)S(1)}, u32[]{:S(2)}, u32[]{:S(2)}) collective-permute-start(s32[64,128]{1,0:T(8,128)S(1)} %get-tuple-element.15), channel_id=1, source_target_pairs={{0,3},{1,13},{2,21},{3,29},{4,31},{5,11},{6,19},{7,27},{8,5},{9,9}... | collective-permute-start | bytes 98312 | tf_op jit(solution)/shard_map/ppermute | solution.py:514
  26.3 13.5 %collective-permute-start.2 = (s32[64,128]{1,0:T(8,128)S(1)}, s32[64,128]{1,0:T(8,128)S(1)}, u32[]{:S(2)}, u32[]{:S(2)}) collective-permute-start(s32[64,128]{1,0:T(8,128)S(1)} %get-tuple-element.16), channel_id=1, source_target_pairs={{0,1},{1,11},{2,19},{3,27},{4,5},{5,7},{6,15},{7,23},{8,31},{9,13}... | collective-permute-start | bytes 98312 | tf_op jit(solution)/shard_map/ppermute | solution.py:514
  35.2 39.7 %copy-start.4 = (bf16[2,512,256]{2,1,0:T(8,128)(2,1)S(1)}, bf16[2,512,256]{2,1,0:T(8,128)(2,1)}, u32[]{:S(2)}) copy-start(bf16[2,512,256]{2,1,0:T(8,128)(2,1)} %constant.27.clone.table_ref) | copy-start | bytes 1572868
  35.2 39.7 %copy-start.10 = (s32[8,640]{1,0:T(8,128)S(1)}, s32[8,640]{1,0:T(8,128)}, u32[]{:S(2)}) copy-start(s32[8,640]{1,0:T(8,128)} %constant.26.clone.lane_ref) | copy-start | bytes 61444
  42.7 35.3 %all-to-all-start = ((f32[32,8,896]{2,1,0:T(8,128)}), f32[32,8,896]{2,1,0:T(8,128)S(1)}, u32[]{:S(2)}, u32[]{:S(2)}) async-start(f32[32,8,896]{2,1,0:T(8,128)} %bitcast.4), calls=%async_computation | async-start | bytes 1835008 | tf_op jit(solution)/shard_map/all_to_all | solution.py:499
  50.9 24.0 %collective-permute-start.3 = (s32[64,128]{1,0:T(8,128)S(1)}, s32[64,128]{1,0:T(8,128)S(1)}, u32[]{:S(2)}, u32[]{:S(2)}) collective-permute-start(s32[64,128]{1,0:T(8,128)S(1)} %get-tuple-element.21), channel_id=1, source_target_pairs={{0,5},{1,9},{2,17},{3,25},{4,3},{5,13},{6,21},{7,29},{8,1},{9,7},{... | collective-permute-start | bytes 98312 | tf_op jit(solution)/shard_map/ppermute | solution.py:514
  57.6 17.3 %collective-permute-start.4 = (s32[64,128]{1,0:T(8,128)S(1)}, s32[64,128]{1,0:T(8,128)S(1)}, u32[]{:S(2)}, u32[]{:S(2)}) collective-permute-start(s32[64,128]{1,0:T(8,128)S(1)} %get-tuple-element.22), channel_id=1, source_target_pairs={{0,0},{1,7},{2,15},{3,23},{4,1},{5,9},{6,17},{7,25},{8,3},{9,11},{... | collective-permute-start | bytes 98312 | tf_op jit(solution)/shard_map/ppermute | solution.py:514
  74.9 3.1 %copy-start.9 = (s32[8,896]{1,0:T(8,128)S(1)}, s32[8,896]{1,0:T(8,128)}, u32[]{:S(2)}) copy-start(s32[8,896]{1,0:T(8,128)} %constant.28.clone.lane_ref) | copy-start | bytes 86020
  77.1 0.9 copy-start.11
  78.0 1.1 copy-start.12
  81.9 49.7 %copy-start.3 = (bf16[2,512,256]{2,1,0:T(8,128)(2,1)S(1)}, bf16[2,512,256]{2,1,0:T(8,128)(2,1)}, u32[]{:S(2)}) copy-start(bf16[2,512,256]{2,1,0:T(8,128)(2,1)} %constant.30.clone.z_ref) | copy-start | bytes 1572868
  81.9 49.7 %copy-start.7 = (bf16[2,128,256]{2,1,0:T(8,128)(2,1)S(1)}, bf16[2,128,256]{2,1,0:T(8,128)(2,1)}, u32[]{:S(2)}) copy-start(bf16[2,128,256]{2,1,0:T(8,128)(2,1)} %constant.29.clone.y_ref) | copy-start | bytes 393220

commit v2 on v1

--- a/solution.py
+++ b/solution.py
@@ -62,14 +62,12 @@
 
 
 @functools.lru_cache(None)
-def lane_rows(count):
-    pieces, size = layout(count)
-    out = np.full((8, size), NO_LINE, np.int32)
-    for kind, _, first, lanes, place in pieces:
-        spots = np.arange(lanes)
-        out[kind, place + spots] = first + spots
-        if kind == 2:
-            out[3, place + spots] = SHARED - 1 - first - spots
+def lane_rows():
+    out = np.full((8, 2 * LANES), NO_LINE, np.int32)
+    for rows in range(2):
+        out[rows, HALF * rows : HALF * rows + WIDE[rows]] = np.arange(WIDE[rows])
+    out[2, LANES : LANES + SHARED] = np.arange(SHARED)
+    out[3, LANES : LANES + SHARED] = np.arange(SHARED)[::-1]
     return out
 
 
@@ -281,14 +279,8 @@
         out_ref[0:BLOCK, tile : tile + LANES] += extra
 
 
-def middle_body(me_ref, device_ref, x_ref, lane_ref, table_ref, *rest):
-    *mask_refs, out_ref, done = rest
-    size = x_ref.shape[1]
-    before = out_ref.shape[1] - size
-    if before:
-        ready_ref, *mask_refs = mask_refs
-        copy = pltpu.make_async_copy(ready_ref, out_ref.at[:, :before], done)
-        copy.start()
+def middle_body(me_ref, device_ref, own_ref, cross_ref, lane_ref, table_ref, *rest):
+    *mask_refs, out_ref = rest
     base = me_ref[0] * 16
     spot = (iota((HALF, LANES), 0) == 0) & (iota((HALF, LANES), 1) == HALF - 1)
     masks = []
@@ -297,42 +289,64 @@
         high = jnp.where(spot, 0.0, pltpu.roll(cells, HALF, 1))
         masks.append(jnp.concatenate([cells, high], axis=0).astype(jnp.bfloat16))
     zero_mask = mask_refs[ZERO_ROUND][0:1, LANES - 1 : LANES].astype(jnp.float32)
-    is_imag = iota((2 * NG, LANES), 0) % BLOCK >= SLAB
+    special = zero_mask / ((1.0 + HALF * HALF / (NG * NG / 16.0)) * float(NG**3))
     kx = iota((NG, LANES), 0)
     signed = jnp.where(kx < HALF, kx, kx - NG)
+    plain = []
+    for lanes in (slice(0, LANES), slice(LANES, 2 * LANES)):
+        cells = jnp.zeros((NG, LANES), jnp.float32)
+        squared = jnp.zeros((1, LANES), jnp.int32)
+        for turn_ in range(4):
+            slot = device_ref[base + 12 + turn_]
+            kz = lane_ref[0:1, lanes]
+            for which in range(1, 4):
+                kz = jnp.where(slot == which, lane_ref[which : which + 1, lanes], kz)
+            ky = device_ref[base + 8 + turn_]
+            chosen = kz < device_ref[base + 4 + turn_]
+            spread = jnp.where((kx == kz) & chosen, 1.0, 0.0).astype(jnp.bfloat16)
+            cells += dot(masks[turn_], spread)
+            squared += jnp.where(chosen, kz * kz + ky * ky, 0)
+        squared = (signed * signed + squared).astype(jnp.float32)
+        plain.append(cells / ((1.0 + squared / (NG * NG / 16.0)) * float(NG**3)))
+
+    lane = iota((NG, LANES), 1)
+    is_imag = iota((2 * NG, LANES), 0) % BLOCK >= SLAB
     forward = both(table_ref, 0, 2 * NG)
     inverse = both(table_ref, 2 * NG, 2 * NG)
-    special = zero_mask / ((1.0 + HALF * HALF / (NG * NG / 16.0)) * float(NG**3))
-    for step in range(0, size, 2 * LANES):
-        values, real, imag = [], [], []
-        for start in range(step, min(step + 2 * LANES, size), LANES):
-            lanes = slice(start, start + LANES)
-            value = x_ref[:, lanes]
-            zero = (lane_ref[0:1, lanes] == 0) & (me_ref[0] == 0)
-            mean = jnp.sum(jnp.where(is_imag, value, 0.0), axis=0, keepdims=True) * (1.0 / NG)
-            values.append(jnp.where(is_imag & zero, mean, value))
-            cells = jnp.zeros((NG, LANES), jnp.float32)
-            squared = jnp.zeros((1, LANES), jnp.int32)
-            for turn_ in range(4):
-                slot = device_ref[base + 12 + turn_]
-                kz = lane_ref[0:1, lanes]
-                for which in range(1, 4):
-                    kz = jnp.where(slot == which, lane_ref[which : which + 1, lanes], kz)
-                ky = device_ref[base + 8 + turn_]
-                chosen = kz < device_ref[base + 4 + turn_]
-                spread = jnp.where((kx == kz) & chosen, 1.0, 0.0).astype(jnp.bfloat16)
-                cells += dot(masks[turn_], spread)
-                squared += jnp.where(chosen, kz * kz + ky * ky, 0)
-            squared = (signed * signed + squared).astype(jnp.float32)
-            weight = cells / ((1.0 + squared / (NG * NG / 16.0)) * float(NG**3))
-            real.append(weight)
-            imag.append(jnp.where((kx == 0) & zero, special, weight))
-        spectrum = dot3(forward, split(beside(values)))
-        weight = jnp.concatenate([beside(real), beside(imag)], axis=0)
-        width = LANES * len(values)
-        out_ref[:, before + step : before + step + width] = dot3(inverse, split(spectrum * weight))
-    if before:
-        copy.wait()
+    offset = 0
+    for count, x_ref in ((3, own_ref), (4, cross_ref)):
+        pieces, size = layout(count)
+        weights = [jnp.zeros((NG, LANES), jnp.float32) for _ in range(size // LANES)]
+        zeros = [[] for _ in weights]
+        for kind, _, first, lanes, place in pieces:
+            tile, start = place // LANES, place % LANES
+            value = lane_roll(plain[kind // 2], start - first - HALF * (kind % 2))
+            inside = (lane >= start) & (lane < start + lanes)
+            weights[tile] = jnp.where(inside, value, weights[tile])
+            if kind == 0:
+                zeros[tile].append(start)
+        for step in range(0, size, 2 * LANES):
+            values, real, imag = [], [], []
+            for tile in range(step // LANES, min(step + 2 * LANES, size) // LANES):
+                value = x_ref[:, LANES * tile : LANES * (tile + 1)]
+                weight = weights[tile]
+                real.append(weight)
+                if zeros[tile]:
+                    at_zero = lane == zeros[tile][0]
+                    for start in zeros[tile][1:]:
+                        at_zero |= lane == start
+                    at_zero &= me_ref[0] == 0
+                    mean = jnp.sum(jnp.where(is_imag, value, 0.0), axis=0, keepdims=True)
+                    value = jnp.where(is_imag & at_zero[0:1], mean * (1.0 / NG), value)
+                    weight = jnp.where((kx == 0) & at_zero, special, weight)
+                values.append(value)
+                imag.append(weight)
+            spectrum = dot3(forward, split(beside(values)))
+            weight = jnp.concatenate([beside(real), beside(imag)], axis=0)
+            place = offset + step
+            width = LANES * len(values)
+            out_ref[:, place : place + width] = dot3(inverse, split(spectrum * weight))
+        offset += size
 
 
 def potentials(count, offset, lines_ref, y_ref, z_ref, width_ref, grids):
@@ -459,7 +473,7 @@
     return call(back_body, (2, SLAB * NG, NG), args, 7, 5 * 10**9, VMEM_LIMIT, "back")
 
 
-def indexed(body, shapes, args, me, flops, name, scratch=(), away=()):
+def indexed(body, shapes, args, me, flops, name):
     vmem = lambda: pl.BlockSpec(memory_space=pltpu.VMEM)
     return pl.pallas_call(
         body,
@@ -467,12 +481,8 @@
         grid_spec=pltpu.PrefetchScalarGridSpec(
             num_scalar_prefetch=2,
             grid=(),
-            in_specs=[
-                pl.BlockSpec(memory_space=pl.ANY) if spot in away else vmem()
-                for spot in range(len(args))
-            ],
+            in_specs=[vmem() for _ in args],
             out_specs=[vmem() for _ in shapes],
-            scratch_shapes=list(scratch),
         ),
         compiler_params=params(),
         cost_estimate=cost(flops, 2 * 10**6),
@@ -480,12 +490,10 @@
     )(me, jnp.asarray(device_table()), *args)
 
 
-def middle(count, values, ready, masks, me, name):
-    args = [values, jnp.asarray(lane_rows(count)), jnp.asarray(pair(x_tables())), *ready, *masks]
-    size = values.shape[1] + sum(part.shape[1] for part in ready)
-    shape = jax.ShapeDtypeStruct((2 * NG, size), jnp.float32)
-    scratch, away = [pltpu.SemaphoreType.DMA], [3] if ready else []
-    return indexed(middle_body, [shape], args, me, 2 * 10**9, name, scratch, away)[0]
+def middle(own, cross, masks, me):
+    args = [own, cross, jnp.asarray(lane_rows()), jnp.asarray(pair(x_tables())), *masks]
+    shape = jax.ShapeDtypeStruct((2 * NG, own.shape[1] + cross.shape[1]), jnp.float32)
+    return indexed(middle_body, [shape], args, me, 4 * 10**9, "middle")[0]
 
 
 def mask_rows(mask, me):
@@ -517,8 +525,7 @@
     sent_cross = ahead(4, cross_products, (own, other), 2 * 10**10, VMEM_LIMIT, "ahead_cross")
     (sent_cross, masks[0], masks[1]) = lax.optimization_barrier((sent_cross, masks[0], masks[1]))
     lines_cross = swap(sent_cross)
-    lines_own = middle(3, lines_own, [], masks, me, "middle_own")
-    lines = swap(middle(4, lines_cross, [lines_own], masks, me, "middle_cross"))
+    lines = swap(middle(lines_own, lines_cross, masks, me))
     return back(own, other, lines).reshape(orbitals.shape)
 
 

time: 136 us -> 132 us (0.971)
  blocking collectives: 49.7 us -> 47.3 us
  waiting for transfers between devices: 24.1 us -> 26.4 us
  Pallas kernels: 17.5 us -> 15.5 us
  local copies, waits for them, and re-layouts: 1.99 us -> 0.05 us
    all_to_all x1, blocking collectives: 49.7 us -> 47.3 us  [swap(): lax.all_to_all(blocks, 'fft', split_axis=0, concat_axis=0, tiled=True)]
    all_to_all x2, waiting for transfers between devices: 2.88 us -> 5.25 us  [swap(): lax.all_to_all(blocks, 'fft', split_axis=0, concat_axis=0, tiled=True)]
    unnamed x26 -> x20, local copies, waits for them, and re-layouts: 1.99 us -> 0.05 us
    pallas_call x3 -> x2, Pallas kernels: 5.74 us -> 3.92 us  [indexed(): pl.pallas_call(body, out_shape=shapes, grid_spec=pltpu.PrefetchScalarGrid...]
  transfers between devices with their start and end apart: 7 -> 7, of which waited for: 3 -> 4; matrix products, arithmetic and copies ran while one was open for 0% -> 0% of each run, Pallas kernels for 8% -> 6%
where the time goes in v2:
time: 132 us
  blocking collectives  47.3 us (36%)
  starting transfers between devices  42.4 us (32%)
  waiting for transfers between devices  26.4 us (20%)
  Pallas kernels  15.5 us (12%)
    all_to_all x1, blocking collectives, swap(): lax.all_to_all(blocks, 'fft', split_axis=0, concat_axis=0, tiled=True)  47.3 us
    all_to_all x2, starting transfers between devices, swap(): lax.all_to_all(blocks, 'fft', split_axis=0, concat_axis=0, tiled=True)  22.1 us
    ppermute x4, waiting for transfers between devices, body(): lax.ppermute(rows, 'fft', pairs)  21.1 us
    ppermute x4, starting transfers between devices, body(): lax.ppermute(rows, 'fft', pairs)  18.4 us
    pallas_call x3, Pallas kernels, call(): pl.pallas_call(body, out_shape=jax.ShapeDtypeStruct(shape, jnp.float32),...  11.6 us
    all_to_all x2, waiting for transfers between devices, swap(): lax.all_to_all(blocks, 'fft', split_axis=0, concat_axis=0, tiled=True)  5.25 us
    pallas_call x2, Pallas kernels, indexed(): pl.pallas_call(body, out_shape=shapes, grid_spec=pltpu.PrefetchScalarGrid...  3.92 us
  transfers between devices with their start and end apart: 7, of which 4 were waited for; matrix products, arithmetic and copies ran while one was open for 0% of the time, Pallas kernels for 6%

profile of v2, /device:TPU:2, one launch (start us, length us, event | category | flops | bytes accessed | tf_op | source)
XLA Modules:
  0.0 131.8 jit_solution(10211003882520505398)
XLA Ops:
  0.0 1.9 %collective-permute-start = (f32[2,4,128,128]{3,2,1,0:T(8,128)}, f32[2,4,128,128]{3,2,1,0:T(8,128)S(1)}, u32[]{:S(2)}, u32[]{:S(2)}) collective-permute-start(f32[2,4,128,128]{3,2,1,0:T(8,128)} %param.12), channel_id=1, source_target_pairs={{0,32},{32,64},{64,96},{96,128},{128,160},{160,192},{192,224},{224... | collective-permute-start | bytes 1572872 | tf_op jit(solution)/shard_map/ppermute | solution.py:514
  1.9 0.0 copy-start
  1.9 0.0 copy-start.1
  1.9 4.3 %ahead_own.1 = f32[256,640]{1,0:T(8,128)} custom-call(f32[2,512,128]{2,1,0:T(8,128)} %bitcast.16, bf16[2,256,128]{2,1,0:T(8,128)(2,1)} %constant.20.clone.refs_1_.refs_2_, bf16[2,512,256]{2,1,0:T(8,128)(2,1)} %constant.21.clone.refs_2_.refs_3_, s32[256,128]{1,0:T(8,128)} %constant.22.clone.refs_3_.refs_4_.width_ref), custom_call_target="tpu_custom_call" | custom-call | flops 20000000000 | bytes 4000000 | tf_op jit(solution)/shard_map/ahead_own/pallas_call | solution.py:451
  6.2 13.9 %all-to-all-start = ((f32[32,8,640]{2,1,0:T(8,128)}), f32[32,8,640]{2,1,0:T(8,128)S(1)}, u32[]{:S(2)}, u32[]{:S(2)}) async-start(f32[32,8,640]{2,1,0:T(8,128)} %bitcast.21), calls=%async_computation | async-start | bytes 1310720 | tf_op jit(solution)/shard_map/all_to_all | solution.py:507
  20.1 0.0 copy-done
  20.1 0.0 copy-done.1
  20.2 0.7 mask_rows.1
  20.8 5.5 %collective-permute-start.1 = (s32[64,128]{1,0:T(8,128)S(1)}, s32[64,128]{1,0:T(8,128)S(1)}, u32[]{:S(2)}, u32[]{:S(2)}) collective-permute-start(s32[64,128]{1,0:T(8,128)S(1)} %get-tuple-element.16), channel_id=1, source_target_pairs={{0,3},{1,13},{2,21},{3,29},{4,31},{5,11},{6,19},{7,27},{8,5},{9,9}... | collective-permute-start | bytes 98312 | tf_op jit(solution)/shard_map/ppermute | solution.py:522
  26.3 5.5 %collective-permute-start.2 = (s32[64,128]{1,0:T(8,128)S(1)}, s32[64,128]{1,0:T(8,128)S(1)}, u32[]{:S(2)}, u32[]{:S(2)}) collective-permute-start(s32[64,128]{1,0:T(8,128)S(1)} %get-tuple-element.17), channel_id=1, source_target_pairs={{0,1},{1,11},{2,19},{3,27},{4,5},{5,7},{6,15},{7,23},{8,31},{9,13}... | collective-permute-start | bytes 98312 | tf_op jit(solution)/shard_map/ppermute | solution.py:522
  31.8 0.0 collective-permute-done
  31.9 0.0 copy-done.2
  31.9 0.0 copy-done.5
  31.9 0.0 copy-done.6
  31.9 0.0 copy-done.8
  31.9 3.3 %ahead_cross.1 = f32[256,896]{1,0:T(8,128)} custom-call(f32[2,512,128]{2,1,0:T(8,128)S(1)} %bitcast.17, f32[2,512,128]{2,1,0:T(8,128)S(1)} %bitcast.19, bf16[2,256,128]{2,1,0:T(8,128)(2,1)S(1)} %copy-done.8, bf16[2,512,256]{2,1,0:T(8,128)(2,1)S(1)} %copy-done.5, s32[256,128]{1,0:T(8,128)S(1)} %copy-done.6), custom_call_target="tpu_custom_call" | custom-call | flops 20000000000 | bytes 4000000 | tf_op jit(solution)/shard_map/ahead_cross/pallas_call | solution.py:451
  35.2 4.6 %collective-permute-done.1.rest_0_ = s32[64,128]{1,0:T(8,128)S(1)} collective-permute-done((s32[64,128]{1,0:T(8,128)S(1)}, s32[64,128]{1,0:T(8,128)S(1)}, u32[]{:S(2)}, u32[]{:S(2)}) %collective-permute-start.1) | collective-permute-done | bytes 32800 | tf_op jit(solution)/shard_map/ppermute | solution.py:522
  39.8 0.0 collective-permute-done.2.rest_1_
  39.8 2.8 %all-to-all-done = f32[32,8,640]{2,1,0:T(8,128)S(1)} async-done(((f32[32,8,640]{2,1,0:T(8,128)}), f32[32,8,640]{2,1,0:T(8,128)S(1)}, u32[]{:S(2)}, u32[]{:S(2)}) %all-to-all-start) | async-done | bytes 655392 | tf_op jit(solution)/shard_map/all_to_all | solution.py:507
  42.6 8.2 %all-to-all-start.1 = ((f32[32,8,896]{2,1,0:T(8,128)}), f32[32,8,896]{2,1,0:T(8,128)S(1)}, u32[]{:S(2)}, u32[]{:S(2)}) async-start(f32[32,8,896]{2,1,0:T(8,128)} %bitcast.6), calls=%async_computation.1 | async-start | bytes 1835008 | tf_op jit(solution)/shard_map/all_to_all | solution.py:507
  50.9 6.7 %collective-permute-start.3 = (s32[64,128]{1,0:T(8,128)S(1)}, s32[64,128]{1,0:T(8,128)S(1)}, u32[]{:S(2)}, u32[]{:S(2)}) collective-permute-start(s32[64,128]{1,0:T(8,128)S(1)} %get-tuple-element.21), channel_id=1, source_target_pairs={{0,5},{1,9},{2,17},{3,25},{4,3},{5,13},{6,21},{7,29},{8,1},{9,7},{... | collective-permute-start | bytes 98312 | tf_op jit(solution)/shard_map/ppermute | solution.py:522
  57.6 0.7 collective-permute-start.4
  58.3 16.6 %collective-permute-done.3.rest_2_ = s32[64,128]{1,0:T(8,128)S(1)} collective-permute-done((s32[64,128]{1,0:T(8,128)S(1)}, s32[64,128]{1,0:T(8,128)S(1)}, u32[]{:S(2)}, u32[]{:S(2)}) %collective-permute-start.3) | collective-permute-done | bytes 32800 | tf_op jit(solution)/shard_map/ppermute | solution.py:522
  74.9 0.0 collective-permute-done.4.rest_3_
  74.9 2.4 %all-to-all-done.1 = f32[32,8,896]{2,1,0:T(8,128)S(1)} async-done(((f32[32,8,896]{2,1,0:T(8,128)}), f32[32,8,896]{2,1,0:T(8,128)S(1)}, u32[]{:S(2)}, u32[]{:S(2)}) %all-to-all-start.1) | async-done | bytes 917536 | tf_op jit(solution)/shard_map/all_to_all | solution.py:507
  77.3 0.0 copy-done.9
  77.3 3.2 %middle.1 = f32[256,1536]{1,0:T(8,128)S(1)} custom-call(s32[1]{0:T(128)} %bitcast.2.me_ref, s32[512]{0:T(512)S(1)} %copy-done.1, f32[256,640]{1,0:T(8,128)S(1)} %bitcast.14, f32[256,896]{1,0:T(8,128)S(1)} %bitcast.13, s32[8,256]{1,0:T(8,128)S(1)} %copy-done.9, bf16[2,512,256]{2,1,0:T(8,128)(2,1)S(1)} %copy-done.4, ...), custom_call_target="tpu_custom_call" | custom-call | flops 4000000000 | bytes 2000000 | tf_op jit(solution)/shard_map/middle/pallas_call | solution.py:478
  80.5 0.0 copy-start.3
  80.5 0.0 copy-start.7
  80.5 47.3 %all_to_all.15 = f32[32,8,1536]{2,1,0:T(8,128)S(1)} all-to-all(f32[32,8,1536]{2,1,0:T(8,128)S(1)} %bitcast.11), channel_id=1, replica_groups=mesh['band'=16,'fft'=32] {'fft'}, dimensions={0} | all-to-all | bytes 3145728 | tf_op jit(solution)/shard_map/all_to_all | solution.py:507
  127.8 0.0 copy-done.3
  127.8 4.0 %back.1 = f32[2,512,128]{2,1,0:T(8,128)} custom-call(f32[2,512,128]{2,1,0:T(8,128)S(1)} %bitcast.18, f32[2,512,128]{2,1,0:T(8,128)S(1)} %bitcast.20, f32[256,1536]{1,0:T(8,128)S(1)} %bitcast.12, bf16[2,128,256]{2,1,0:T(8,128)(2,1)S(1)} %copy-done.7, bf16[2,512,256]{2,1,0:T(8,128)(2,1)S(1)} %copy-done.3, s32[256,128]{1,0:T(8,128)S(1)} %copy-done.6), custom_call_target="tpu_custom_call" | custom-call | flops 5000000000 | bytes 4000000 | tf_op jit(solution)/shard_map/back/pallas_call | solution.py:451
  (8 shorter events, 0.0 us)
Async XLA Ops:
  0.0 31.8 %collective-permute-start = (f32[2,4,128,128]{3,2,1,0:T(8,128)}, f32[2,4,128,128]{3,2,1,0:T(8,128)S(1)}, u32[]{:S(2)}, u32[]{:S(2)}) collective-permute-start(f32[2,4,128,128]{3,2,1,0:T(8,128)} %param.12), channel_id=1, source_target_pairs={{0,32},{32,64},{64,96},{96,128},{128,160},{160,192},{192,224},{224... | collective-permute-start | bytes 1572872 | tf_op jit(solution)/shard_map/ppermute | solution.py:514
  1.9 18.2 %copy-start = (s32[128,4,128]{2,1,0:T(4,128)S(1)}, s32[128,4,128]{2,1,0:T(4,128)}, u32[]{:S(2)}) copy-start(s32[128,4,128]{2,1,0:T(4,128)} %param.13) | copy-start | bytes 786436
  1.9 18.2 %copy-start.1 = (s32[512]{0:T(512)S(1)}, s32[512]{0:T(512)}, u32[]{:S(2)}) copy-start(s32[512]{0:T(512)} %constant.23.clone.device_ref) | copy-start | bytes 6148
  6.2 25.6 %copy-start.2 = (f32[2,4,128,128]{3,2,1,0:T(8,128)S(1)}, f32[2,4,128,128]{3,2,1,0:T(8,128)}, u32[]{:S(2)}) copy-start(f32[2,4,128,128]{3,2,1,0:T(8,128)} %param.12) | copy-start | bytes 1572868
  6.2 25.6 %copy-start.5 = (bf16[2,512,256]{2,1,0:T(8,128)(2,1)S(1)}, bf16[2,512,256]{2,1,0:T(8,128)(2,1)}, u32[]{:S(2)}) copy-start(bf16[2,512,256]{2,1,0:T(8,128)(2,1)} %constant.21.clone.refs_2_.refs_3_) | copy-start | bytes 1572868
  6.2 25.7 %copy-start.6 = (s32[256,128]{1,0:T(8,128)S(1)}, s32[256,128]{1,0:T(8,128)}, u32[]{:S(2)}) copy-start(s32[256,128]{1,0:T(8,128)} %constant.22.clone.refs_3_.refs_4_.width_ref) | copy-start | bytes 393220
  6.2 25.7 %copy-start.8 = (bf16[2,256,128]{2,1,0:T(8,128)(2,1)S(1)}, bf16[2,256,128]{2,1,0:T(8,128)(2,1)}, u32[]{:S(2)}) copy-start(bf16[2,256,128]{2,1,0:T(8,128)(2,1)} %constant.20.clone.refs_1_.refs_2_) | copy-start | bytes 393220
  6.2 36.4 %all-to-all-start = ((f32[32,8,640]{2,1,0:T(8,128)}), f32[32,8,640]{2,1,0:T(8,128)S(1)}, u32[]{:S(2)}, u32[]{:S(2)}) async-start(f32[32,8,640]{2,1,0:T(8,128)} %bitcast.21), calls=%async_computation | async-start | bytes 1310720 | tf_op jit(solution)/shard_map/all_to_all | solution.py:507
  20.8 18.9 %collective-permute-start.1 = (s32[64,128]{1,0:T(8,128)S(1)}, s32[64,128]{1,0:T(8,128)S(1)}, u32[]{:S(2)}, u32[]{:S(2)}) collective-permute-start(s32[64,128]{1,0:T(8,128)S(1)} %get-tuple-element.16), channel_id=1, source_target_pairs={{0,3},{1,13},{2,21},{3,29},{4,31},{5,11},{6,19},{7,27},{8,5},{9,9}... | collective-permute-start | bytes 98312 | tf_op jit(solution)/shard_map/ppermute | solution.py:522
  26.3 13.4 %collective-permute-start.2 = (s32[64,128]{1,0:T(8,128)S(1)}, s32[64,128]{1,0:T(8,128)S(1)}, u32[]{:S(2)}, u32[]{:S(2)}) collective-permute-start(s32[64,128]{1,0:T(8,128)S(1)} %get-tuple-element.17), channel_id=1, source_target_pairs={{0,1},{1,11},{2,19},{3,27},{4,5},{5,7},{6,15},{7,23},{8,31},{9,13}... | collective-permute-start | bytes 98312 | tf_op jit(solution)/shard_map/ppermute | solution.py:522
  35.2 42.1 %copy-start.4 = (bf16[2,512,256]{2,1,0:T(8,128)(2,1)S(1)}, bf16[2,512,256]{2,1,0:T(8,128)(2,1)}, u32[]{:S(2)}) copy-start(bf16[2,512,256]{2,1,0:T(8,128)(2,1)} %constant.25.clone.table_ref) | copy-start | bytes 1572868
  35.2 42.1 %copy-start.9 = (s32[8,256]{1,0:T(8,128)S(1)}, s32[8,256]{1,0:T(8,128)}, u32[]{:S(2)}) copy-start(s32[8,256]{1,0:T(8,128)} %constant.24.clone.lane_ref) | copy-start | bytes 24580
  42.6 34.6 %all-to-all-start.1 = ((f32[32,8,896]{2,1,0:T(8,128)}), f32[32,8,896]{2,1,0:T(8,128)S(1)}, u32[]{:S(2)}, u32[]{:S(2)}) async-start(f32[32,8,896]{2,1,0:T(8,128)} %bitcast.6), calls=%async_computation.1 | async-start | bytes 1835008 | tf_op jit(solution)/shard_map/all_to_all | solution.py:507
  50.9 24.0 %collective-permute-start.3 = (s32[64,128]{1,0:T(8,128)S(1)}, s32[64,128]{1,0:T(8,128)S(1)}, u32[]{:S(2)}, u32[]{:S(2)}) collective-permute-start(s32[64,128]{1,0:T(8,128)S(1)} %get-tuple-element.21), channel_id=1, source_target_pairs={{0,5},{1,9},{2,17},{3,25},{4,3},{5,13},{6,21},{7,29},{8,1},{9,7},{... | collective-permute-start | bytes 98312 | tf_op jit(solution)/shard_map/ppermute | solution.py:522
  57.6 17.3 %collective-permute-start.4 = (s32[64,128]{1,0:T(8,128)S(1)}, s32[64,128]{1,0:T(8,128)S(1)}, u32[]{:S(2)}, u32[]{:S(2)}) collective-permute-start(s32[64,128]{1,0:T(8,128)S(1)} %get-tuple-element.22), channel_id=1, source_target_pairs={{0,0},{1,7},{2,15},{3,23},{4,1},{5,9},{6,17},{7,25},{8,3},{9,11},{... | collective-permute-start | bytes 98312 | tf_op jit(solution)/shard_map/ppermute | solution.py:522
  80.5 47.3 %copy-start.3 = (bf16[2,512,256]{2,1,0:T(8,128)(2,1)S(1)}, bf16[2,512,256]{2,1,0:T(8,128)(2,1)}, u32[]{:S(2)}) copy-start(bf16[2,512,256]{2,1,0:T(8,128)(2,1)} %constant.27.clone.z_ref) | copy-start | bytes 1572868
  80.5 47.3 %copy-start.7 = (bf16[2,128,256]{2,1,0:T(8,128)(2,1)S(1)}, bf16[2,128,256]{2,1,0:T(8,128)(2,1)}, u32[]{:S(2)}) copy-start(bf16[2,128,256]{2,1,0:T(8,128)(2,1)} %constant.26.clone.y_ref) | copy-start | bytes 393220

commit v3 on v2

--- a/solution.py
+++ b/solution.py
@@ -26,9 +26,19 @@
     return min(HALF, math.isqrt(HALF * HALF - ky * ky) + 1)
 
 
+N_LO = 4
+
+
 def row_sets():
-    order = sorted(range(-HALF, HALF), key=lambda k: (abs(k), -k))
-    return [order[:32], order[32:64], order[64:96], order[:95:-1]]
+    sets = [[], [], [], []]
+    for device in range(N_FFT):
+        lo, z = divmod(device, N_FFT // N_LO)
+        run = SLAB * z + lo
+        plain = sorted((run, run - 32), key=abs)
+        shared = sorted((run + 32, run - 64), key=abs)
+        for rows, ky in zip(sets, plain + shared):
+            rows.append(ky)
+    return sets
 
 
 KY = row_sets()
@@ -131,34 +141,19 @@
 
 @functools.lru_cache(None)
 def mask_rounds():
-    edges = {source: [] for source in range(N_FFT)}
-    for device in range(N_FFT):
-        for rows in range(4):
-            index = KY[rows][device] % NG
-            edges[index // SLAB].append((device, index % SLAB, rows))
     rounds = []
-    for _ in range(SLAB):
-        taken = {}
-
-        def place(source, seen):
-            for edge in edges[source]:
-                if edge[0] in seen:
-                    continue
-                seen.add(edge[0])
-                if edge[0] not in taken or place(taken[edge[0]][0], seen):
-                    taken[edge[0]] = (source, edge)
-                    return True
-            return False
-
-        for source in range(N_FFT):
-            assert place(source, set())
+    step = N_FFT // N_LO
+    for turn_ in range(N_LO):
         pairs, local, slot = [], [0] * N_FFT, [0] * N_FFT
-        for device, (source, edge) in taken.items():
-            edges[source].remove(edge)
+        for device in range(N_FFT):
+            lo, z = divmod(device, step)
+            source = (lo ^ turn_) * step + z
             pairs.append((source, device))
-            local[source] = edge[1]
-            slot[device] = edge[2]
-        rounds.append((tuple(sorted(pairs)), tuple(local), tuple(slot)))
+            local[source] = lo
+            row = SLAB * source + lo
+            ky = row if row < HALF else row - NG
+            slot[device] = [KY[rows][device] for rows in range(4)].index(ky)
+        rounds.append((tuple(pairs), tuple(local), tuple(slot)))
     return tuple(rounds)
 
 
@@ -224,6 +219,12 @@
     inputs = refs[:n_in]
     y_ref, z_ref, width_ref, out_ref, *grids = refs[n_in:]
     pieces, size = layout(count)
+    before = out_ref.shape[1] - size
+    if before:
+        *inputs, ready_ref = inputs
+        *grids, done = grids
+        copy = pltpu.make_async_copy(ready_ref, out_ref.at[:, :before], done)
+        copy.start()
     fields = products_of(inputs)
     is_imag = iota((2 * NG, LANES), 0) % BLOCK >= SLAB
     sides = {}
@@ -263,7 +264,8 @@
             old = jnp.zeros_like(value)
         tiles[place // LANES] = jnp.where((lane >= start) & (lane < start + lanes), value, old)
     for tile, value in enumerate(tiles):
-        out_ref[:, LANES * tile : LANES * (tile + 1)] = value
+        place = before + LANES * tile
+        out_ref[:, place : place + LANES] = value
     row, column = iota((BLOCK, LANES), 0), iota((BLOCK, LANES), 1)
     sign = (1 - 2 * (iota((1, NG), 1) % 2)).astype(jnp.float32)
     for kind, field, _, _, place in pieces:
@@ -275,11 +277,13 @@
             cells = jnp.sum(cells, axis=0, keepdims=True) * sign
             value = jnp.sum(cells, axis=1, keepdims=True)
             extra = jnp.where((row == SLAB + x) & (column == place % LANES), value, extra)
-        tile = place // LANES * LANES
+        tile = before + place // LANES * LANES
         out_ref[0:BLOCK, tile : tile + LANES] += extra
-
-
-def middle_body(me_ref, device_ref, own_ref, cross_ref, lane_ref, table_ref, *rest):
+    if before:
+        copy.wait()
+
+
+def weight_body(me_ref, device_ref, lane_ref, *rest):
     *mask_refs, out_ref = rest
     base = me_ref[0] * 16
     spot = (iota((HALF, LANES), 0) == 0) & (iota((HALF, LANES), 1) == HALF - 1)
@@ -291,9 +295,10 @@
     zero_mask = mask_refs[ZERO_ROUND][0:1, LANES - 1 : LANES].astype(jnp.float32)
     special = zero_mask / ((1.0 + HALF * HALF / (NG * NG / 16.0)) * float(NG**3))
     kx = iota((NG, LANES), 0)
+    lane = iota((NG, LANES), 1)
     signed = jnp.where(kx < HALF, kx, kx - NG)
-    plain = []
-    for lanes in (slice(0, LANES), slice(LANES, 2 * LANES)):
+    for kind in range(2):
+        lanes = slice(LANES * kind, LANES * (kind + 1))
         cells = jnp.zeros((NG, LANES), jnp.float32)
         squared = jnp.zeros((1, LANES), jnp.int32)
         for turn_ in range(4):
@@ -307,16 +312,23 @@
             cells += dot(masks[turn_], spread)
             squared += jnp.where(chosen, kz * kz + ky * ky, 0)
         squared = (signed * signed + squared).astype(jnp.float32)
-        plain.append(cells / ((1.0 + squared / (NG * NG / 16.0)) * float(NG**3)))
-
-    lane = iota((NG, LANES), 1)
+        weight = cells / ((1.0 + squared / (NG * NG / 16.0)) * float(NG**3))
+        out_ref[:NG, lanes] = weight
+        if kind == 0:
+            weight = jnp.where((kx == 0) & (lane == 0) & (me_ref[0] == 0), special, weight)
+        out_ref[NG:, lanes] = weight
+
+
+def middle_body(me_ref, x_ref, weight_ref, table_ref, out_ref):
+    plain = [weight_ref[:, LANES * kind : LANES * (kind + 1)] for kind in range(2)]
+    lane = iota((2 * NG, LANES), 1)
     is_imag = iota((2 * NG, LANES), 0) % BLOCK >= SLAB
     forward = both(table_ref, 0, 2 * NG)
     inverse = both(table_ref, 2 * NG, 2 * NG)
     offset = 0
-    for count, x_ref in ((3, own_ref), (4, cross_ref)):
+    for count in (3, 4):
         pieces, size = layout(count)
-        weights = [jnp.zeros((NG, LANES), jnp.float32) for _ in range(size // LANES)]
+        weights = [jnp.zeros((2 * NG, LANES), jnp.float32) for _ in range(size // LANES)]
         zeros = [[] for _ in weights]
         for kind, _, first, lanes, place in pieces:
             tile, start = place // LANES, place % LANES
@@ -326,23 +338,21 @@
             if kind == 0:
                 zeros[tile].append(start)
         for step in range(0, size, 2 * LANES):
-            values, real, imag = [], [], []
-            for tile in range(step // LANES, min(step + 2 * LANES, size) // LANES):
-                value = x_ref[:, LANES * tile : LANES * (tile + 1)]
-                weight = weights[tile]
-                real.append(weight)
+            values = []
+            tiles = range(step // LANES, min(step + 2 * LANES, size) // LANES)
+            for tile in tiles:
+                place = offset + LANES * tile
+                value = x_ref[:, place : place + LANES]
                 if zeros[tile]:
                     at_zero = lane == zeros[tile][0]
                     for start in zeros[tile][1:]:
                         at_zero |= lane == start
                     at_zero &= me_ref[0] == 0
                     mean = jnp.sum(jnp.where(is_imag, value, 0.0), axis=0, keepdims=True)
-                    value = jnp.where(is_imag & at_zero[0:1], mean * (1.0 / NG), value)
-                    weight = jnp.where((kx == 0) & at_zero, special, weight)
+                    value = jnp.where(is_imag & at_zero, mean * (1.0 / NG), value)
                 values.append(value)
-                imag.append(weight)
             spectrum = dot3(forward, split(beside(values)))
-            weight = jnp.concatenate([beside(real), beside(imag)], axis=0)
+            weight = beside([weights[tile] for tile in tiles])
             place = offset + step
             width = LANES * len(values)
             out_ref[:, place : place + width] = dot3(inverse, split(spectrum * weight))
@@ -398,14 +408,17 @@
     return plane_of
 
 
-def back_body(own_ref, other_ref, lines_ref, y_ref, z_ref, width_ref, out_ref, *grids):
+def back_body(
+    core_ref, own_ref, near_ref, far_ref, lines_ref, y_ref, z_ref, width_ref, out_ref, *grids
+):
+    partner = partners(core_ref, near_ref, far_ref)
     tables = (lines_ref, y_ref, z_ref, width_ref)
     own_plane = potentials(3, 0, *tables, grids[:3])
     cross_plane = potentials(4, layout(3)[1], *tables, grids[3:])
     for x in range(SLAB):
         plane = slice(NG * x, NG * x + NG)
         own = [own_ref[band, plane, :] for band in range(2)]
-        other = [other_ref[band, plane, :] for band in range(2)]
+        other = [partner(band, plane) for band in range(2)]
         first, mixed, second = own_plane(x)
         cross = cross_plane(x)
         total = first * own[0] + mixed * own[1] + (cross[0] * other[0] + cross[1] * other[1])
@@ -414,18 +427,23 @@
         out_ref[1, plane, :] = -0.5 * total
 
 
-def product(left, i, right, j):
-    return lambda plane: left[i, plane, :] * right[j, plane, :]
-
-
 def own_products(refs):
     (own,) = refs
-    return [product(own, 0, own, 0), product(own, 0, own, 1), product(own, 1, own, 1)]
+    mixed = lambda i, j: lambda plane: own[i, plane, :] * own[j, plane, :]
+    return [mixed(0, 0), mixed(0, 1), mixed(1, 1)]
+
+
+def partners(core_ref, near_ref, far_ref):
+    return lambda band, plane: jnp.where(
+        core_ref[0] == 1, near_ref[band, plane, :], far_ref[band, plane, :]
+    )
 
 
 def cross_products(refs):
-    own, other = refs
-    return [product(own, b, other, j) for b in range(2) for j in range(2)]
+    core, own, near, far = refs
+    other = partners(core, near, far)
+    mixed = lambda b, j: lambda plane: own[b, plane, :] * other(j, plane)
+    return [mixed(b, j) for b in range(2) for j in range(2)]
 
 
 def mask_body(me_ref, device_ref, mask_ref, *out_refs):
@@ -447,39 +465,54 @@
     return pl.CostEstimate(flops=flops, bytes_accessed=moved, transcendentals=0)
 
 
-def call(body, shape, args, fields, flops, limit, name):
+def call(body, shape, args, fields, flops, limit, name, kinds=None, extra=()):
+    spaces = {"v": pltpu.VMEM, "s": pltpu.SMEM, "a": pl.ANY}
+    kinds = kinds + "v" * (len(args) - len(kinds)) if kinds else "v" * len(args)
     return pl.pallas_call(
         body,
         out_shape=jax.ShapeDtypeStruct(shape, jnp.float32),
-        in_specs=[pl.BlockSpec(memory_space=pltpu.VMEM) for _ in args],
+        in_specs=[pl.BlockSpec(memory_space=spaces[kind]) for kind in kinds],
         out_specs=pl.BlockSpec(memory_space=pltpu.VMEM),
-        scratch_shapes=[pltpu.VMEM((ROWS_ALL, NG), jnp.float32) for _ in range(fields)],
+        scratch_shapes=[pltpu.VMEM((ROWS_ALL, NG), jnp.float32) for _ in range(fields)] + list(extra),
         compiler_params=params(limit),
         cost_estimate=cost(flops, 4 * 10**6),
         name=name,
     )(*args)
 
 
-def ahead(count, products_of, grids, flops, limit, name):
+def ahead_tables():
     tables = (pair(y_table()), pair(z_ahead()), shared_width())
-    args = [*grids, *(jnp.asarray(table) for table in tables)]
-    body = functools.partial(ahead_body, count, products_of, len(grids))
-    return call(body, (2 * NG, layout(count)[1]), args, count, flops, limit, name)
-
-
-def back(own, other, values):
+    return [jnp.asarray(table) for table in tables]
+
+
+def ahead_own(own):
+    body = functools.partial(ahead_body, 3, own_products, 1)
+    shape = (2 * NG, layout(3)[1])
+    return call(body, shape, [own, *ahead_tables()], 3, 2 * 10**10, VMEM_MOST, "ahead_own")
+
+
+def ahead_cross(core, own, near, far, ready):
+    body = functools.partial(ahead_body, 4, cross_products, 5)
+    shape = (2 * NG, layout(3)[1] + layout(4)[1])
+    args = [core, own, near, far, ready, *ahead_tables()]
+    semaphore = [pltpu.SemaphoreType.DMA]
+    return call(body, shape, args, 4, 5 * 10**9, VMEM_LIMIT, "ahead_cross", "svvva", semaphore)
+
+
+def back(core, own, near, far, values):
     tables = (pair(y_table().T), pair(z_back()), shared_width())
-    args = [own, other, values, *(jnp.asarray(table) for table in tables)]
-    return call(back_body, (2, SLAB * NG, NG), args, 7, 5 * 10**9, VMEM_LIMIT, "back")
-
-
-def indexed(body, shapes, args, me, flops, name):
+    args = [core, own, near, far, values, *(jnp.asarray(table) for table in tables)]
+    shape = (2, SLAB * NG, NG)
+    return call(back_body, shape, args, 7, 5 * 10**9, VMEM_LIMIT, "back", "s")
+
+
+def indexed(body, shapes, scalars, args, flops, name):
     vmem = lambda: pl.BlockSpec(memory_space=pltpu.VMEM)
     return pl.pallas_call(
         body,
         out_shape=shapes,
         grid_spec=pltpu.PrefetchScalarGridSpec(
-            num_scalar_prefetch=2,
+            num_scalar_prefetch=len(scalars),
             grid=(),
             in_specs=[vmem() for _ in args],
             out_specs=[vmem() for _ in shapes],
@@ -487,18 +520,26 @@
         compiler_params=params(),
         cost_estimate=cost(flops, 2 * 10**6),
         name=name,
-    )(me, jnp.asarray(device_table()), *args)
-
-
-def middle(own, cross, masks, me):
-    args = [own, cross, jnp.asarray(lane_rows()), jnp.asarray(pair(x_tables())), *masks]
-    shape = jax.ShapeDtypeStruct((2 * NG, own.shape[1] + cross.shape[1]), jnp.float32)
-    return indexed(middle_body, [shape], args, me, 4 * 10**9, "middle")[0]
+    )(*scalars, *args)
+
+
+def weights_of(masks, me):
+    shape = jax.ShapeDtypeStruct((2 * NG, 2 * LANES), jnp.float32)
+    scalars = [me, jnp.asarray(device_table())]
+    args = [jnp.asarray(lane_rows()), *masks]
+    return indexed(weight_body, [shape], scalars, args, 10**9, "weights")[0]
+
+
+def middle(values, weights, me):
+    args = [values, weights, jnp.asarray(pair(x_tables()))]
+    shape = jax.ShapeDtypeStruct(values.shape, jnp.float32)
+    return indexed(middle_body, [shape], [me], args, 4 * 10**9, "middle")[0]
 
 
 def mask_rows(mask, me):
     shapes = [jax.ShapeDtypeStruct((HALF, NG), jnp.int32)] * SLAB
-    return indexed(mask_body, shapes, [mask.reshape(NG * SLAB, NG)], me, 10**6, "mask_rows")
+    scalars = [me, jnp.asarray(device_table())]
+    return indexed(mask_body, shapes, scalars, [mask.reshape(NG * SLAB, NG)], 10**6, "mask_rows")
 
 
 def swap(values):
@@ -510,23 +551,21 @@
 
 def body(orbitals, mask):
     me = lax.axis_index("fft").astype(jnp.int32)[None]
+    core = (lax.axis_index("band") % 2).astype(jnp.int32)[None]
     count = lax.axis_size("band")
-    other = lax.ppermute(orbitals, "band", [(i, (i + 1) % count) for i in range(count)])
-    own = orbitals.reshape(2, SLAB * NG, NG)
-    other = other.reshape(2, SLAB * NG, NG)
-
-    sent_own = ahead(3, own_products, (own,), 2 * 10**10, VMEM_MOST, "ahead_own")
-    sent_own, mask = lax.optimization_barrier((sent_own, mask))
-    lines_own = swap(sent_own)
-    masks = [
-        lax.ppermute(rows, "fft", pairs)
-        for rows, (pairs, _, _) in zip(mask_rows(mask, me), mask_rounds())
-    ]
-    sent_cross = ahead(4, cross_products, (own, other), 2 * 10**10, VMEM_LIMIT, "ahead_cross")
-    (sent_cross, masks[0], masks[1]) = lax.optimization_barrier((sent_cross, masks[0], masks[1]))
-    lines_cross = swap(sent_cross)
-    lines = swap(middle(lines_own, lines_cross, masks, me))
-    return back(own, other, lines).reshape(orbitals.shape)
+    near = lax.ppermute(orbitals, "band", [(i, i ^ 1) for i in range(count)])
+    far = lax.ppermute(near, "band", [(i, (i + 2) % count) for i in range(0, count, 2)])
+    shape = (2, SLAB * NG, NG)
+    own, near, far = orbitals.reshape(shape), near.reshape(shape), far.reshape(shape)
+
+    sent = ahead_cross(core, own, near, far, ahead_own(own))
+    sent, mask = lax.optimization_barrier((sent, mask))
+    lines = swap(sent)
+    masks = list(mask_rows(mask, me))
+    for turn_ in range(1, N_LO):
+        masks[turn_] = lax.ppermute(masks[turn_], "fft", mask_rounds()[turn_][0])
+    lines = swap(middle(lines, weights_of(masks, me), me))
+    return back(core, own, near, far, lines).reshape(orbitals.shape)
 
 
 def solution(mesh):

time: 132 us -> 121 us (0.917)
  blocking collectives: 47.3 us -> 41 us
  starting transfers between devices: 42.4 us -> 37 us
  waiting for transfers between devices: 26.4 us -> 22.4 us
  local copies, waits for them, and re-layouts: 0.05 us -> 3.83 us
    all_to_all x1, blocking collectives: 47.3 us -> 41 us  [swap(): lax.all_to_all(blocks, 'fft', split_axis=0, concat_axis=0, tiled=True)]
    all_to_all x2 -> x1, waiting for transfers between devices: 5.25 us -> 0.01 us  [swap(): lax.all_to_all(blocks, 'fft', split_axis=0, concat_axis=0, tiled=True)]
    all_to_all x2 -> x1, starting transfers between devices: 22.1 us -> 17.2 us  [swap(): lax.all_to_all(blocks, 'fft', split_axis=0, concat_axis=0, tiled=True)]
    unnamed x20 -> x26, local copies, waits for them, and re-layouts: 0.05 us -> 3.83 us
    pallas_call x2 -> x3, Pallas kernels: 3.92 us -> 4.06 us  [indexed(): pl.pallas_call(body, out_shape=shapes, grid_spec=pltpu.PrefetchScalarGrid...]
  transfers between devices with their start and end apart: 7 -> 6, of which waited for: 4 -> 4; matrix products, arithmetic and copies ran while one was open for 0% -> 0% of each run, Pallas kernels for 6% -> 5%
where the time goes in v3:
time: 121 us
  blocking collectives  41 us (34%)
  starting transfers between devices  37 us (31%)
  waiting for transfers between devices  22.4 us (19%)
  Pallas kernels  16.2 us (13%)
  local copies, waits for them, and re-layouts  3.83 us (3%)
    all_to_all x1, blocking collectives, swap(): lax.all_to_all(blocks, 'fft', split_axis=0, concat_axis=0, tiled=True)  41 us
    all_to_all x1, starting transfers between devices, swap(): lax.all_to_all(blocks, 'fft', split_axis=0, concat_axis=0, tiled=True)  17.2 us
    ppermute x3, waiting for transfers between devices, body(): masks[turn_] = lax.ppermute(masks[turn_], 'fft', mask_rounds()[turn_][0])  14.7 us
    pallas_call x3, Pallas kernels, call(): pl.pallas_call(body, out_shape=jax.ShapeDtypeStruct(shape, jnp.float32),...  12.2 us
    ppermute x3, starting transfers between devices, body(): masks[turn_] = lax.ppermute(masks[turn_], 'fft', mask_rounds()[turn_][0])  10.1 us
    ppermute x1, starting transfers between devices, body(): lax.ppermute(near, 'band', [(i, (i + 2) % count) for i in range(0, count,...  7.72 us
    ppermute x1, waiting for transfers between devices, body(): lax.ppermute(near, 'band', [(i, (i + 2) % count) for i in range(0, count,...  5.6 us
    pallas_call x3, Pallas kernels, indexed(): pl.pallas_call(body, out_shape=shapes, grid_spec=pltpu.PrefetchScalarGrid...  4.06 us
  transfers between devices with their start and end apart: 6, of which 4 were waited for; matrix products, arithmetic and copies ran while one was open for 0% of the time, Pallas kernels for 5%

profile of v3, /device:TPU:2, one launch (start us, length us, event | category | flops | bytes accessed | tf_op | source)
XLA Modules:
  0.0 120.6 jit_solution(12068284699429184255)
XLA Ops:
  0.0 1.9 %collective-permute-start = (f32[2,4,128,128]{3,2,1,0:T(8,128)}, f32[2,4,128,128]{3,2,1,0:T(8,128)S(1)}, u32[]{:S(2)}, u32[]{:S(2)}) collective-permute-start(f32[2,4,128,128]{3,2,1,0:T(8,128)} %param.12), channel_id=1, source_target_pairs={{0,32},{32,0},{64,96},{96,64},{128,160},{160,128},{192,224},{224,1... | collective-permute-start | bytes 1572872 | tf_op jit(solution)/shard_map/ppermute | solution.py:556
  1.9 2.1 %collective-permute-done = f32[2,4,128,128]{3,2,1,0:T(8,128)S(1)} collective-permute-done((f32[2,4,128,128]{3,2,1,0:T(8,128)}, f32[2,4,128,128]{3,2,1,0:T(8,128)S(1)}, u32[]{:S(2)}, u32[]{:S(2)}) %collective-permute-start) | collective-permute-done | bytes 524320 | tf_op jit(solution)/shard_map/ppermute | solution.py:556
  4.0 7.7 %collective-permute-start.1 = (f32[2,4,128,128]{3,2,1,0:T(8,128)S(1)}, f32[2,4,128,128]{3,2,1,0:T(8,128)S(1)}, u32[]{:S(2)}, u32[]{:S(2)}) collective-permute-start(f32[2,4,128,128]{3,2,1,0:T(8,128)S(1)} %collective-permute-done), channel_id=1, source_target_pairs={{0,64},{64,128},{128,192},{192,256},{256,320},{320,384},{384,448},... | collective-permute-start | bytes 1572872 | tf_op jit(solution)/shard_map/ppermute | solution.py:557
  11.7 0.0 copy-start.2
  11.7 0.0 copy-start.5
  11.8 0.0 copy-start.6
  11.8 0.0 copy-start.8
  11.8 4.3 %ahead_own.1.refs_4_ = f32[256,640]{1,0:T(8,128)} custom-call(f32[2,512,128]{2,1,0:T(8,128)} %bitcast.15, bf16[2,256,128]{2,1,0:T(8,128)(2,1)} %constant.38.clone.refs_1_.refs_5_, bf16[2,512,256]{2,1,0:T(8,128)(2,1)} %constant.39.clone.refs_2_.refs_6_, s32[256,128]{1,0:T(8,128)} %constant.40.clone.refs_3_.refs_7_.width_ref), custom_call_target="tpu_custom_call" | custom-call | flops 20000000000 | bytes 4000000 | tf_op jit(solution)/shard_map/ahead_own/pallas_call | solution.py:471
  16.1 5.6 %collective-permute-done.1 = f32[2,4,128,128]{3,2,1,0:T(8,128)S(1)} collective-permute-done((f32[2,4,128,128]{3,2,1,0:T(8,128)S(1)}, f32[2,4,128,128]{3,2,1,0:T(8,128)S(1)}, u32[]{:S(2)}, u32[]{:S(2)}) %collective-permute-start.1) | collective-permute-done | bytes 524320 | tf_op jit(solution)/shard_map/ppermute | solution.py:557
  21.7 1.1 copy-done.12
  22.8 3.7 %ahead_cross.1 = f32[256,1536]{1,0:T(8,128)} custom-call(s32[1]{0:T(128)} %bitcast.refs_0_.core_ref, f32[2,512,128]{2,1,0:T(8,128)S(1)} %bitcast.16, f32[2,512,128]{2,1,0:T(8,128)S(1)} %bitcast.18, f32[2,512,128]{2,1,0:T(8,128)S(1)} %bitcast.20, f32[256,640]{1,0:T(8,128)S(1)} %copy-done.12, bf16[2,256,128]{2,1,0:T(8,128)(2,1)S(1)} %copy-done.8, ...), custom_call_target="tpu_custom_call" | custom-call | flops 5000000000 | bytes 4000000 | tf_op jit(solution)/shard_map/ahead_cross/pallas_call | solution.py:471
  26.5 0.0 copy-start
  26.5 0.0 copy-start.1
  26.5 0.0 copy-start.9
  26.5 17.2 %all-to-all-start = ((f32[32,8,1536]{2,1,0:T(8,128)}), f32[32,8,1536]{2,1,0:T(8,128)S(1)}, u32[]{:S(2)}, u32[]{:S(2)}) async-start(f32[32,8,1536]{2,1,0:T(8,128)} %bitcast.5), calls=%async_computation | async-start | bytes 3145728 | tf_op jit(solution)/shard_map/all_to_all | solution.py:548
  43.8 0.7 mask_rows.1
  44.5 3.7 %collective-permute-start.2 = (s32[64,128]{1,0:T(8,128)S(1)}, s32[64,128]{1,0:T(8,128)S(1)}, u32[]{:S(2)}, u32[]{:S(2)}) collective-permute-start(s32[64,128]{1,0:T(8,128)S(1)} %get-tuple-element.14), channel_id=1, source_target_pairs={{8,0},{9,1},{10,2},{11,3},{12,4},{13,5},{14,6},{15,7},{0,8},{1,9},... | collective-permute-start | bytes 98312 | tf_op jit(solution)/shard_map/ppermute | solution.py:566
  48.2 4.3 %collective-permute-start.3 = (s32[64,128]{1,0:T(8,128)S(1)}, s32[64,128]{1,0:T(8,128)S(1)}, u32[]{:S(2)}, u32[]{:S(2)}) collective-permute-start(s32[64,128]{1,0:T(8,128)S(1)} %get-tuple-element.15), channel_id=1, source_target_pairs={{16,0},{17,1},{18,2},{19,3},{20,4},{21,5},{22,6},{23,7},{24,8},{25... | collective-permute-start | bytes 98312 | tf_op jit(solution)/shard_map/ppermute | solution.py:566
  52.5 2.1 %collective-permute-start.4 = (s32[64,128]{1,0:T(8,128)S(1)}, s32[64,128]{1,0:T(8,128)S(1)}, u32[]{:S(2)}, u32[]{:S(2)}) collective-permute-start(s32[64,128]{1,0:T(8,128)S(1)} %get-tuple-element.16), channel_id=1, source_target_pairs={{24,0},{25,1},{26,2},{27,3},{28,4},{29,5},{30,6},{31,7},{16,8},{17... | collective-permute-start | bytes 98312 | tf_op jit(solution)/shard_map/ppermute | solution.py:566
  54.6 6.5 %collective-permute-done.2.rest_1_ = s32[64,128]{1,0:T(8,128)S(1)} collective-permute-done((s32[64,128]{1,0:T(8,128)S(1)}, s32[64,128]{1,0:T(8,128)S(1)}, u32[]{:S(2)}, u32[]{:S(2)}) %collective-permute-start.2) | collective-permute-done | bytes 32800 | tf_op jit(solution)/shard_map/ppermute | solution.py:566
  61.1 8.2 %collective-permute-done.3.rest_2_ = s32[64,128]{1,0:T(8,128)S(1)} collective-permute-done((s32[64,128]{1,0:T(8,128)S(1)}, s32[64,128]{1,0:T(8,128)S(1)}, u32[]{:S(2)}, u32[]{:S(2)}) %collective-permute-start.3) | collective-permute-done | bytes 32800 | tf_op jit(solution)/shard_map/ppermute | solution.py:566
  69.3 0.0 collective-permute-done.4.rest_3_
  69.3 0.8 weights.1.weight_ref
  70.2 0.7 copy-done.10
  70.9 0.0 all-to-all-done
  70.9 1.0 copy-done.4
  71.9 0.9 copy-done.11
  72.9 2.5 %middle.1 = f32[256,1536]{1,0:T(8,128)S(1)} custom-call(s32[1]{0:T(128)} %bitcast.4.me_ref, f32[256,1536]{1,0:T(8,128)S(1)} %bitcast.11, f32[256,256]{1,0:T(8,128)S(1)} %copy-done.11, bf16[2,512,256]{2,1,0:T(8,128)(2,1)S(1)} %copy-done.4), custom_call_target="tpu_custom_call" | custom-call | flops 4000000000 | bytes 2000000 | tf_op jit(solution)/shard_map/middle/pallas_call | solution.py:511
  75.4 0.0 copy-start.3
  75.4 0.0 copy-start.7
  75.4 41.0 %all_to_all.10 = f32[32,8,1536]{2,1,0:T(8,128)S(1)} all-to-all(f32[32,8,1536]{2,1,0:T(8,128)S(1)} %bitcast.13), channel_id=1, replica_groups=mesh['band'=16,'fft'=32] {'fft'}, dimensions={0} | all-to-all | bytes 3145728 | tf_op jit(solution)/shard_map/all_to_all | solution.py:548
  116.4 4.2 %back.1 = f32[2,512,128]{2,1,0:T(8,128)} custom-call(s32[1]{0:T(128)} %bitcast.refs_0_.core_ref, f32[2,512,128]{2,1,0:T(8,128)S(1)} %bitcast.17, f32[2,512,128]{2,1,0:T(8,128)S(1)} %bitcast.19, f32[2,512,128]{2,1,0:T(8,128)S(1)} %bitcast.21, f32[256,1536]{1,0:T(8,128)S(1)} %bitcast.12, bf16[2,128,256]{2,1,0:T(8,128)(2,1)S(1)} %copy-done.7, ...), custom_call_target="tpu_custom_call" | custom-call | flops 5000000000 | bytes 4000000 | tf_op jit(solution)/shard_map/back/pallas_call | solution.py:471
  (13 shorter events, 0.0 us)
Async XLA Ops:
  0.0 4.0 %collective-permute-start = (f32[2,4,128,128]{3,2,1,0:T(8,128)}, f32[2,4,128,128]{3,2,1,0:T(8,128)S(1)}, u32[]{:S(2)}, u32[]{:S(2)}) collective-permute-start(f32[2,4,128,128]{3,2,1,0:T(8,128)} %param.12), channel_id=1, source_target_pairs={{0,32},{32,0},{64,96},{96,64},{128,160},{160,128},{192,224},{224,1... | collective-permute-start | bytes 1572872 | tf_op jit(solution)/shard_map/ppermute | solution.py:556
  4.0 17.7 %collective-permute-start.1 = (f32[2,4,128,128]{3,2,1,0:T(8,128)S(1)}, f32[2,4,128,128]{3,2,1,0:T(8,128)S(1)}, u32[]{:S(2)}, u32[]{:S(2)}) collective-permute-start(f32[2,4,128,128]{3,2,1,0:T(8,128)S(1)} %collective-permute-done), channel_id=1, source_target_pairs={{0,64},{64,128},{128,192},{192,256},{256,320},{320,384},{384,448},... | collective-permute-start | bytes 1572872 | tf_op jit(solution)/shard_map/ppermute | solution.py:557
  11.7 10.0 %copy-start.2 = (f32[2,4,128,128]{3,2,1,0:T(8,128)S(1)}, f32[2,4,128,128]{3,2,1,0:T(8,128)}, u32[]{:S(2)}) copy-start(f32[2,4,128,128]{3,2,1,0:T(8,128)} %param.12) | copy-start | bytes 1572868
  11.7 10.0 %copy-start.5 = (bf16[2,512,256]{2,1,0:T(8,128)(2,1)S(1)}, bf16[2,512,256]{2,1,0:T(8,128)(2,1)}, u32[]{:S(2)}) copy-start(bf16[2,512,256]{2,1,0:T(8,128)(2,1)} %constant.39.clone.refs_2_.refs_6_) | copy-start | bytes 1572868
  11.8 9.9 %copy-start.6 = (s32[256,128]{1,0:T(8,128)S(1)}, s32[256,128]{1,0:T(8,128)}, u32[]{:S(2)}) copy-start(s32[256,128]{1,0:T(8,128)} %constant.40.clone.refs_3_.refs_7_.width_ref) | copy-start | bytes 393220
  11.8 9.9 %copy-start.8 = (bf16[2,256,128]{2,1,0:T(8,128)(2,1)S(1)}, bf16[2,256,128]{2,1,0:T(8,128)(2,1)}, u32[]{:S(2)}) copy-start(bf16[2,256,128]{2,1,0:T(8,128)(2,1)} %constant.38.clone.refs_1_.refs_5_) | copy-start | bytes 393220
  21.7 1.1 copy-start.12
  26.5 17.3 %copy-start = (s32[128,4,128]{2,1,0:T(4,128)S(1)}, s32[128,4,128]{2,1,0:T(4,128)}, u32[]{:S(2)}) copy-start(s32[128,4,128]{2,1,0:T(4,128)} %param.13) | copy-start | bytes 786436
  26.5 17.3 %copy-start.1 = (s32[512]{0:T(512)S(1)}, s32[512]{0:T(512)}, u32[]{:S(2)}) copy-start(s32[512]{0:T(512)} %constant.41.clone.device_ref) | copy-start | bytes 6148
  26.5 42.8 %copy-start.9 = (s32[8,256]{1,0:T(8,128)S(1)}, s32[8,256]{1,0:T(8,128)}, u32[]{:S(2)}) copy-start(s32[8,256]{1,0:T(8,128)} %constant.42.clone.lane_ref) | copy-start | bytes 24580
  26.5 44.4 %all-to-all-start = ((f32[32,8,1536]{2,1,0:T(8,128)}), f32[32,8,1536]{2,1,0:T(8,128)S(1)}, u32[]{:S(2)}, u32[]{:S(2)}) async-start(f32[32,8,1536]{2,1,0:T(8,128)} %bitcast.5), calls=%async_computation | async-start | bytes 3145728 | tf_op jit(solution)/shard_map/all_to_all | solution.py:548
  44.5 16.6 %collective-permute-start.2 = (s32[64,128]{1,0:T(8,128)S(1)}, s32[64,128]{1,0:T(8,128)S(1)}, u32[]{:S(2)}, u32[]{:S(2)}) collective-permute-start(s32[64,128]{1,0:T(8,128)S(1)} %get-tuple-element.14), channel_id=1, source_target_pairs={{8,0},{9,1},{10,2},{11,3},{12,4},{13,5},{14,6},{15,7},{0,8},{1,9},... | collective-permute-start | bytes 98312 | tf_op jit(solution)/shard_map/ppermute | solution.py:566
  48.2 21.1 %collective-permute-start.3 = (s32[64,128]{1,0:T(8,128)S(1)}, s32[64,128]{1,0:T(8,128)S(1)}, u32[]{:S(2)}, u32[]{:S(2)}) collective-permute-start(s32[64,128]{1,0:T(8,128)S(1)} %get-tuple-element.15), channel_id=1, source_target_pairs={{16,0},{17,1},{18,2},{19,3},{20,4},{21,5},{22,6},{23,7},{24,8},{25... | collective-permute-start | bytes 98312 | tf_op jit(solution)/shard_map/ppermute | solution.py:566
  52.5 16.8 %collective-permute-start.4 = (s32[64,128]{1,0:T(8,128)S(1)}, s32[64,128]{1,0:T(8,128)S(1)}, u32[]{:S(2)}, u32[]{:S(2)}) collective-permute-start(s32[64,128]{1,0:T(8,128)S(1)} %get-tuple-element.16), channel_id=1, source_target_pairs={{24,0},{25,1},{26,2},{27,3},{28,4},{29,5},{30,6},{31,7},{16,8},{17... | collective-permute-start | bytes 98312 | tf_op jit(solution)/shard_map/ppermute | solution.py:566
  70.2 0.7 copy-start.10
  70.9 1.0 copy-start.4
  71.9 0.9 copy-start.11
  75.4 41.0 %copy-start.3 = (bf16[2,512,256]{2,1,0:T(8,128)(2,1)S(1)}, bf16[2,512,256]{2,1,0:T(8,128)(2,1)}, u32[]{:S(2)}) copy-start(bf16[2,512,256]{2,1,0:T(8,128)(2,1)} %constant.45.clone.z_ref) | copy-start | bytes 1572868
  75.4 41.0 %copy-start.7 = (bf16[2,128,256]{2,1,0:T(8,128)(2,1)S(1)}, bf16[2,128,256]{2,1,0:T(8,128)(2,1)}, u32[]{:S(2)}) copy-start(bf16[2,128,256]{2,1,0:T(8,128)(2,1)} %constant.44.clone.y_ref) | copy-start | bytes 393220

commit v4 on v3

--- a/solution.py
+++ b/solution.py
@@ -215,16 +215,10 @@
     return lax.broadcasted_iota(jnp.int32, shape, dim)
 
 
-def ahead_body(count, products_of, n_in, *refs):
+def ahead_body(count, before, products_of, n_in, *refs):
     inputs = refs[:n_in]
-    y_ref, z_ref, width_ref, out_ref, *grids = refs[n_in:]
+    y_ref, z_ref, width_ref, sent_ref, *grids, out_ref, done = refs[n_in:]
     pieces, size = layout(count)
-    before = out_ref.shape[1] - size
-    if before:
-        *inputs, ready_ref = inputs
-        *grids, done = grids
-        copy = pltpu.make_async_copy(ready_ref, out_ref.at[:, :before], done)
-        copy.start()
     fields = products_of(inputs)
     is_imag = iota((2 * NG, LANES), 0) % BLOCK >= SLAB
     sides = {}
@@ -263,23 +257,30 @@
         if old is None:
             old = jnp.zeros_like(value)
         tiles[place // LANES] = jnp.where((lane >= start) & (lane < start + lanes), value, old)
-    for tile, value in enumerate(tiles):
-        place = before + LANES * tile
-        out_ref[:, place : place + LANES] = value
     row, column = iota((BLOCK, LANES), 0), iota((BLOCK, LANES), 1)
     sign = (1 - 2 * (iota((1, NG), 1) % 2)).astype(jnp.float32)
+    extras = {}
     for kind, field, _, _, place in pieces:
         if kind:
             continue
-        extra = jnp.zeros((BLOCK, LANES), jnp.float32)
+        extra = extras.get(place // LANES, jnp.zeros((BLOCK, LANES), jnp.float32))
         for x in range(SLAB):
             cells = fields[field](slice(NG * x, NG * x + NG))
             cells = jnp.sum(cells, axis=0, keepdims=True) * sign
             value = jnp.sum(cells, axis=1, keepdims=True)
             extra = jnp.where((row == SLAB + x) & (column == place % LANES), value, extra)
-        tile = before + place // LANES * LANES
-        out_ref[0:BLOCK, tile : tile + LANES] += extra
-    if before:
+        extras[place // LANES] = extra
+    copies = []
+    for tile, value in enumerate(tiles):
+        lanes = slice(LANES * tile, LANES * (tile + 1))
+        out_ref[:, lanes] = value
+        if tile in extras:
+            out_ref[0:BLOCK, lanes] += extras[tile]
+        start = before + LANES * tile
+        target = sent_ref.at[:, start : start + LANES]
+        copies.append(pltpu.make_async_copy(out_ref.at[:, lanes], target, done.at[tile]))
+        copies[-1].start()
+    for copy in copies:
         copy.wait()
 
 
@@ -440,7 +441,7 @@
 
 
 def cross_products(refs):
-    core, own, near, far = refs
+    core, own, near, far, _ = refs
     other = partners(core, near, far)
     mixed = lambda b, j: lambda plane: own[b, plane, :] * other(j, plane)
     return [mixed(b, j) for b in range(2) for j in range(2)]
@@ -465,15 +466,20 @@
     return pl.CostEstimate(flops=flops, bytes_accessed=moved, transcendentals=0)
 
 
-def call(body, shape, args, fields, flops, limit, name, kinds=None, extra=()):
+def call(body, shape, args, fields, flops, limit, name, kinds="", sent=None):
     spaces = {"v": pltpu.VMEM, "s": pltpu.SMEM, "a": pl.ANY}
-    kinds = kinds + "v" * (len(args) - len(kinds)) if kinds else "v" * len(args)
+    kinds += "v" * (len(args) - len(kinds))
+    scratch = [pltpu.VMEM((ROWS_ALL, NG), jnp.float32) for _ in range(fields)]
+    if sent:
+        scratch += [pltpu.VMEM((2 * NG, sent), jnp.float32)]
+        scratch += [pltpu.SemaphoreType.DMA((sent // LANES,))]
     return pl.pallas_call(
         body,
         out_shape=jax.ShapeDtypeStruct(shape, jnp.float32),
         in_specs=[pl.BlockSpec(memory_space=spaces[kind]) for kind in kinds],
-        out_specs=pl.BlockSpec(memory_space=pltpu.VMEM),
-        scratch_shapes=[pltpu.VMEM((ROWS_ALL, NG), jnp.float32) for _ in range(fields)] + list(extra),
+        out_specs=pl.BlockSpec(memory_space=pl.ANY if sent else pltpu.VMEM),
+        scratch_shapes=scratch,
+        input_output_aliases={kinds.index("a"): 0} if "a" in kinds else {},
         compiler_params=params(limit),
         cost_estimate=cost(flops, 4 * 10**6),
         name=name,
@@ -485,18 +491,22 @@
     return [jnp.asarray(table) for table in tables]
 
 
+OWN_LANES, CROSS_LANES = layout(3)[1], layout(4)[1]
+SENT_SHAPE = (2 * NG, OWN_LANES + CROSS_LANES)
+
+
 def ahead_own(own):
-    body = functools.partial(ahead_body, 3, own_products, 1)
-    shape = (2 * NG, layout(3)[1])
-    return call(body, shape, [own, *ahead_tables()], 3, 2 * 10**10, VMEM_MOST, "ahead_own")
+    body = functools.partial(ahead_body, 3, 0, own_products, 1)
+    args = [own, *ahead_tables()]
+    return call(body, SENT_SHAPE, args, 3, 2 * 10**10, VMEM_MOST, "ahead_own", sent=OWN_LANES)
 
 
 def ahead_cross(core, own, near, far, ready):
-    body = functools.partial(ahead_body, 4, cross_products, 5)
-    shape = (2 * NG, layout(3)[1] + layout(4)[1])
+    body = functools.partial(ahead_body, 4, OWN_LANES, cross_products, 5)
     args = [core, own, near, far, ready, *ahead_tables()]
-    semaphore = [pltpu.SemaphoreType.DMA]
-    return call(body, shape, args, 4, 5 * 10**9, VMEM_LIMIT, "ahead_cross", "svvva", semaphore)
+    return call(
+        body, SENT_SHAPE, args, 4, 5 * 10**9, VMEM_MOST, "ahead_cross", "svvva", CROSS_LANES
+    )
 
 
 def back(core, own, near, far, values):

time: 121 us -> 121 us (level)
  the two profiles are of different devices: /device:TPU:2 before, /device:TPU:44 now
where the time goes in v4:
time: 121 us; the launch traced here: 120 us
  blocking collectives  45.8 us (38%)
  waiting for transfers between devices  28.7 us (24%)
  starting transfers between devices  27.3 us (23%)
  Pallas kernels  17.1 us (14%)
    all_to_all x1, blocking collectives, swap(): lax.all_to_all(blocks, 'fft', split_axis=0, concat_axis=0, tiled=True)  45.8 us
    ppermute x3, waiting for transfers between devices, body(): masks[turn_] = lax.ppermute(masks[turn_], 'fft', mask_rounds()[turn_][0])  13.4 us
    pallas_call x3, Pallas kernels, call(): pl.pallas_call(body, out_shape=jax.ShapeDtypeStruct(shape, jnp.float32),...  13 us
    ppermute x1, waiting for transfers between devices, body(): lax.ppermute(near, 'band', [(i, (i + 2) % count) for i in range(0, count,...  12.8 us
    all_to_all x1, starting transfers between devices, swap(): lax.all_to_all(blocks, 'fft', split_axis=0, concat_axis=0, tiled=True)  12.6 us
    ppermute x3, starting transfers between devices, body(): masks[turn_] = lax.ppermute(masks[turn_], 'fft', mask_rounds()[turn_][0])  9.21 us
    pallas_call x3, Pallas kernels, indexed(): pl.pallas_call(body, out_shape=shapes, grid_spec=pltpu.PrefetchScalarGrid...  4.05 us
    ppermute x1, starting transfers between devices, body(): lax.ppermute(near, 'band', [(i, (i + 2) % count) for i in range(0, count,...  3.54 us
  transfers between devices with their start and end apart: 6, of which 6 were waited for; matrix products, arithmetic and copies ran while one was open for 0% of the time, Pallas kernels for 5%

profile of v4, /device:TPU:44, one launch (start us, length us, event | category | flops | bytes accessed | tf_op | source)
XLA Modules:
  0.0 120.0 jit_solution(956119601650891402)
XLA Ops:
  0.0 1.9 %collective-permute-start = (f32[2,4,128,128]{3,2,1,0:T(8,128)}, f32[2,4,128,128]{3,2,1,0:T(8,128)S(1)}, u32[]{:S(2)}, u32[]{:S(2)}) collective-permute-start(f32[2,4,128,128]{3,2,1,0:T(8,128)} %param.12), channel_id=1, source_target_pairs={{0,32},{32,0},{64,96},{96,64},{128,160},{160,128},{192,224},{224,1... | collective-permute-start | bytes 1572872 | tf_op jit(solution)/shard_map/ppermute | solution.py:566
  1.9 2.1 %collective-permute-done = f32[2,4,128,128]{3,2,1,0:T(8,128)S(1)} collective-permute-done((f32[2,4,128,128]{3,2,1,0:T(8,128)}, f32[2,4,128,128]{3,2,1,0:T(8,128)S(1)}, u32[]{:S(2)}, u32[]{:S(2)}) %collective-permute-start) | collective-permute-done | bytes 524320 | tf_op jit(solution)/shard_map/ppermute | solution.py:566
  4.0 3.5 %collective-permute-start.1 = (f32[2,4,128,128]{3,2,1,0:T(8,128)S(1)}, f32[2,4,128,128]{3,2,1,0:T(8,128)S(1)}, u32[]{:S(2)}, u32[]{:S(2)}) collective-permute-start(f32[2,4,128,128]{3,2,1,0:T(8,128)S(1)} %collective-permute-done), channel_id=1, source_target_pairs={{0,64},{64,128},{128,192},{192,256},{256,320},{320,384},{384,448},... | collective-permute-start | bytes 1572872 | tf_op jit(solution)/shard_map/ppermute | solution.py:567
  7.6 4.2 %ahead_own.1.refs_4_ = f32[256,1536]{1,0:T(8,128)} custom-call(f32[2,512,128]{2,1,0:T(8,128)} %bitcast.15, bf16[2,256,128]{2,1,0:T(8,128)(2,1)} %constant.38.clone.refs_1_.refs_5_, bf16[2,512,256]{2,1,0:T(8,128)(2,1)} %constant.39.clone.refs_2_.refs_6_, s32[256,128]{1,0:T(8,128)} %constant.40.clone.refs_3_.refs_7_.width_ref), custom_call_target="tpu_custom_call" | custom-call | flops 20000000000 | bytes 4000000 | tf_op jit(solution)/shard_map/ahead_own/pallas_call | solution.py:476
  11.8 0.0 copy-done.3
  11.8 12.8 %collective-permute-done.1 = f32[2,4,128,128]{3,2,1,0:T(8,128)S(1)} collective-permute-done((f32[2,4,128,128]{3,2,1,0:T(8,128)S(1)}, f32[2,4,128,128]{3,2,1,0:T(8,128)S(1)}, u32[]{:S(2)}, u32[]{:S(2)}) %collective-permute-start.1) | collective-permute-done | bytes 524320 | tf_op jit(solution)/shard_map/ppermute | solution.py:567
  24.6 0.8 copy-done.5
  25.4 4.8 %ahead_cross.1 = f32[256,1536]{1,0:T(8,128)} custom-call(s32[1]{0:T(128)} %bitcast.refs_0_.core_ref, f32[2,512,128]{2,1,0:T(8,128)} %bitcast.16, f32[2,512,128]{2,1,0:T(8,128)} %bitcast.18, f32[2,512,128]{2,1,0:T(8,128)} %bitcast.20, f32[256,1536]{1,0:T(8,128)} %ahead_own.1.refs_4_, ...), custom_call_target="tpu_custom_call", output_to_operand_aliasing={{}: (4, {})} | custom-call | flops 5000000000 | bytes 4000000 | tf_op jit(solution)/shard_map/ahead_cross/pallas_call | solution.py:476
  30.2 0.0 copy-start
  30.2 0.0 copy-start.1
  30.2 0.0 copy-start.11
  30.2 12.6 %all-to-all-start = ((f32[32,8,1536]{2,1,0:T(8,128)}), f32[32,8,1536]{2,1,0:T(8,128)S(1)}, u32[]{:S(2)}, u32[]{:S(2)}) async-start(f32[32,8,1536]{2,1,0:T(8,128)} %bitcast.22), calls=%async_computation | async-start | bytes 3145728 | tf_op jit(solution)/shard_map/all_to_all | solution.py:558
  42.9 0.7 mask_rows.1
  43.6 2.1 %collective-permute-start.2 = (s32[64,128]{1,0:T(8,128)S(1)}, s32[64,128]{1,0:T(8,128)S(1)}, u32[]{:S(2)}, u32[]{:S(2)}) collective-permute-start(s32[64,128]{1,0:T(8,128)S(1)} %get-tuple-element.14), channel_id=1, source_target_pairs={{8,0},{9,1},{10,2},{11,3},{12,4},{13,5},{14,6},{15,7},{0,8},{1,9},... | collective-permute-start | bytes 98312 | tf_op jit(solution)/shard_map/ppermute | solution.py:576
  45.7 4.6 %collective-permute-start.3 = (s32[64,128]{1,0:T(8,128)S(1)}, s32[64,128]{1,0:T(8,128)S(1)}, u32[]{:S(2)}, u32[]{:S(2)}) collective-permute-start(s32[64,128]{1,0:T(8,128)S(1)} %get-tuple-element.15), channel_id=1, source_target_pairs={{16,0},{17,1},{18,2},{19,3},{20,4},{21,5},{22,6},{23,7},{24,8},{25... | collective-permute-start | bytes 98312 | tf_op jit(solution)/shard_map/ppermute | solution.py:576
  50.3 2.5 %collective-permute-start.4 = (s32[64,128]{1,0:T(8,128)S(1)}, s32[64,128]{1,0:T(8,128)S(1)}, u32[]{:S(2)}, u32[]{:S(2)}) collective-permute-start(s32[64,128]{1,0:T(8,128)S(1)} %get-tuple-element.16), channel_id=1, source_target_pairs={{24,0},{25,1},{26,2},{27,3},{28,4},{29,5},{30,6},{31,7},{16,8},{17... | collective-permute-start | bytes 98312 | tf_op jit(solution)/shard_map/ppermute | solution.py:576
  52.8 4.8 %collective-permute-done.2.rest_1_ = s32[64,128]{1,0:T(8,128)S(1)} collective-permute-done((s32[64,128]{1,0:T(8,128)S(1)}, s32[64,128]{1,0:T(8,128)S(1)}, u32[]{:S(2)}, u32[]{:S(2)}) %collective-permute-start.2) | collective-permute-done | bytes 32800 | tf_op jit(solution)/shard_map/ppermute | solution.py:576
  57.6 5.8 %collective-permute-done.3.rest_2_ = s32[64,128]{1,0:T(8,128)S(1)} collective-permute-done((s32[64,128]{1,0:T(8,128)S(1)}, s32[64,128]{1,0:T(8,128)S(1)}, u32[]{:S(2)}, u32[]{:S(2)}) %collective-permute-start.3) | collective-permute-done | bytes 32800 | tf_op jit(solution)/shard_map/ppermute | solution.py:576
  63.5 2.8 %collective-permute-done.4.rest_3_ = s32[64,128]{1,0:T(8,128)S(1)} collective-permute-done((s32[64,128]{1,0:T(8,128)S(1)}, s32[64,128]{1,0:T(8,128)S(1)}, u32[]{:S(2)}, u32[]{:S(2)}) %collective-permute-start.4) | collective-permute-done | bytes 32800 | tf_op jit(solution)/shard_map/ppermute | solution.py:576
  66.3 0.0 copy-done.11
  66.3 0.8 weights.1.weight_ref
  67.1 0.4 all-to-all-done
  67.5 2.5 %middle.1 = f32[256,1536]{1,0:T(8,128)S(1)} custom-call(s32[1]{0:T(128)} %bitcast.4.me_ref, f32[256,1536]{1,0:T(8,128)S(1)} %bitcast.11, f32[256,256]{1,0:T(8,128)S(1)} %weights.1.weight_ref, bf16[2,512,256]{2,1,0:T(8,128)(2,1)S(1)} %copy-done.8), custom_call_target="tpu_custom_call" | custom-call | flops 4000000000 | bytes 2000000 | tf_op jit(solution)/shard_map/middle/pallas_call | solution.py:521
  70.1 0.0 copy-start.2
  70.1 0.0 copy-start.4
  70.1 0.0 copy-start.6
  70.1 0.0 copy-start.7
  70.1 0.0 copy-start.9
  70.1 0.0 copy-start.10
  70.2 45.8 %all_to_all.10 = f32[32,8,1536]{2,1,0:T(8,128)S(1)} all-to-all(f32[32,8,1536]{2,1,0:T(8,128)S(1)} %bitcast.13), channel_id=1, replica_groups=mesh['band'=16,'fft'=32] {'fft'}, dimensions={0} | all-to-all | bytes 3145728 | tf_op jit(solution)/shard_map/all_to_all | solution.py:558
  116.0 0.0 copy-done.6
  116.0 4.0 %back.1 = f32[2,512,128]{2,1,0:T(8,128)} custom-call(s32[1]{0:T(128)} %bitcast.refs_0_.core_ref, f32[2,512,128]{2,1,0:T(8,128)S(1)} %bitcast.17, f32[2,512,128]{2,1,0:T(8,128)S(1)} %bitcast.19, f32[2,512,128]{2,1,0:T(8,128)S(1)} %bitcast.21, f32[256,1536]{1,0:T(8,128)S(1)} %bitcast.12, bf16[2,128,256]{2,1,0:T(8,128)(2,1)S(1)} %copy-done.10, ...), custom_call_target="tpu_custom_call" | custom-call | flops 5000000000 | bytes 4000000 | tf_op jit(solution)/shard_map/back/pallas_call | solution.py:476
  (11 shorter events, 0.0 us)
Async XLA Ops:
  0.0 4.0 %collective-permute-start = (f32[2,4,128,128]{3,2,1,0:T(8,128)}, f32[2,4,128,128]{3,2,1,0:T(8,128)S(1)}, u32[]{:S(2)}, u32[]{:S(2)}) collective-permute-start(f32[2,4,128,128]{3,2,1,0:T(8,128)} %param.12), channel_id=1, source_target_pairs={{0,32},{32,0},{64,96},{96,64},{128,160},{160,128},{192,224},{224,1... | collective-permute-start | bytes 1572872 | tf_op jit(solution)/shard_map/ppermute | solution.py:566
  4.0 7.8 %copy-start.3 = (f32[2,4,128,128]{3,2,1,0:T(8,128)}, f32[2,4,128,128]{3,2,1,0:T(8,128)S(1)}, u32[]{:S(2)}) copy-start(f32[2,4,128,128]{3,2,1,0:T(8,128)S(1)} %collective-permute-done) | copy-start | bytes 1572868
  4.0 20.6 %collective-permute-start.1 = (f32[2,4,128,128]{3,2,1,0:T(8,128)S(1)}, f32[2,4,128,128]{3,2,1,0:T(8,128)S(1)}, u32[]{:S(2)}, u32[]{:S(2)}) collective-permute-start(f32[2,4,128,128]{3,2,1,0:T(8,128)S(1)} %collective-permute-done), channel_id=1, source_target_pairs={{0,64},{64,128},{128,192},{192,256},{256,320},{320,384},{384,448},... | collective-permute-start | bytes 1572872 | tf_op jit(solution)/shard_map/ppermute | solution.py:567
  24.6 0.8 copy-start.5
  30.2 12.7 %copy-start = (s32[128,4,128]{2,1,0:T(4,128)S(1)}, s32[128,4,128]{2,1,0:T(4,128)}, u32[]{:S(2)}) copy-start(s32[128,4,128]{2,1,0:T(4,128)} %param.13) | copy-start | bytes 786436
  30.2 12.7 %copy-start.1 = (s32[512]{0:T(512)S(1)}, s32[512]{0:T(512)}, u32[]{:S(2)}) copy-start(s32[512]{0:T(512)} %constant.41.clone.device_ref) | copy-start | bytes 6148
  30.2 36.0 %copy-start.11 = (s32[8,256]{1,0:T(8,128)S(1)}, s32[8,256]{1,0:T(8,128)}, u32[]{:S(2)}) copy-start(s32[8,256]{1,0:T(8,128)} %constant.42.clone.lane_ref) | copy-start | bytes 24580
  30.2 37.3 %all-to-all-start = ((f32[32,8,1536]{2,1,0:T(8,128)}), f32[32,8,1536]{2,1,0:T(8,128)S(1)}, u32[]{:S(2)}, u32[]{:S(2)}) async-start(f32[32,8,1536]{2,1,0:T(8,128)} %bitcast.22), calls=%async_computation | async-start | bytes 3145728 | tf_op jit(solution)/shard_map/all_to_all | solution.py:558
  43.6 14.1 %collective-permute-start.2 = (s32[64,128]{1,0:T(8,128)S(1)}, s32[64,128]{1,0:T(8,128)S(1)}, u32[]{:S(2)}, u32[]{:S(2)}) collective-permute-start(s32[64,128]{1,0:T(8,128)S(1)} %get-tuple-element.14), channel_id=1, source_target_pairs={{8,0},{9,1},{10,2},{11,3},{12,4},{13,5},{14,6},{15,7},{0,8},{1,9},... | collective-permute-start | bytes 98312 | tf_op jit(solution)/shard_map/ppermute | solution.py:576
  45.7 17.8 %collective-permute-start.3 = (s32[64,128]{1,0:T(8,128)S(1)}, s32[64,128]{1,0:T(8,128)S(1)}, u32[]{:S(2)}, u32[]{:S(2)}) collective-permute-start(s32[64,128]{1,0:T(8,128)S(1)} %get-tuple-element.15), channel_id=1, source_target_pairs={{16,0},{17,1},{18,2},{19,3},{20,4},{21,5},{22,6},{23,7},{24,8},{25... | collective-permute-start | bytes 98312 | tf_op jit(solution)/shard_map/ppermute | solution.py:576
  50.3 15.9 %collective-permute-start.4 = (s32[64,128]{1,0:T(8,128)S(1)}, s32[64,128]{1,0:T(8,128)S(1)}, u32[]{:S(2)}, u32[]{:S(2)}) collective-permute-start(s32[64,128]{1,0:T(8,128)S(1)} %get-tuple-element.16), channel_id=1, source_target_pairs={{24,0},{25,1},{26,2},{27,3},{28,4},{29,5},{30,6},{31,7},{16,8},{17... | collective-permute-start | bytes 98312 | tf_op jit(solution)/shard_map/ppermute | solution.py:576
  66.3 1.3 %copy-start.8 = (bf16[2,512,256]{2,1,0:T(8,128)(2,1)S(1)}, bf16[2,512,256]{2,1,0:T(8,128)(2,1)}, u32[]{:S(2)}) copy-start(bf16[2,512,256]{2,1,0:T(8,128)(2,1)} %constant.43.clone.table_ref) | copy-start | bytes 1572868
  70.1 45.9 %copy-start.2 = (f32[2,4,128,128]{3,2,1,0:T(8,128)S(1)}, f32[2,4,128,128]{3,2,1,0:T(8,128)}, u32[]{:S(2)}) copy-start(f32[2,4,128,128]{3,2,1,0:T(8,128)} %param.12) | copy-start | bytes 1572868
  70.1 45.9 %copy-start.4 = (f32[2,4,128,128]{3,2,1,0:T(8,128)S(1)}, f32[2,4,128,128]{3,2,1,0:T(8,128)}, u32[]{:S(2)}) copy-start(f32[2,4,128,128]{3,2,1,0:T(8,128)} %copy-done.3) | copy-start | bytes 1572868
  70.1 45.9 %copy-start.6 = (f32[2,4,128,128]{3,2,1,0:T(8,128)S(1)}, f32[2,4,128,128]{3,2,1,0:T(8,128)}, u32[]{:S(2)}) copy-start(f32[2,4,128,128]{3,2,1,0:T(8,128)} %copy-done.5) | copy-start | bytes 1572868
  70.1 45.9 %copy-start.7 = (bf16[2,512,256]{2,1,0:T(8,128)(2,1)S(1)}, bf16[2,512,256]{2,1,0:T(8,128)(2,1)}, u32[]{:S(2)}) copy-start(bf16[2,512,256]{2,1,0:T(8,128)(2,1)} %constant.45.clone.z_ref) | copy-start | bytes 1572868
  70.1 45.9 %copy-start.9 = (s32[256,128]{1,0:T(8,128)S(1)}, s32[256,128]{1,0:T(8,128)}, u32[]{:S(2)}) copy-start(s32[256,128]{1,0:T(8,128)} %constant.40.clone.refs_3_.refs_7_.width_ref) | copy-start | bytes 393220
  70.1 45.9 %copy-start.10 = (bf16[2,128,256]{2,1,0:T(8,128)(2,1)S(1)}, bf16[2,128,256]{2,1,0:T(8,128)(2,1)}, u32[]{:S(2)}) copy-start(bf16[2,128,256]{2,1,0:T(8,128)(2,1)} %constant.44.clone.y_ref) | copy-start | bytes 393220

commit v5 on v4

--- a/solution.py
+++ b/solution.py
@@ -410,8 +410,10 @@
 
 
 def back_body(
-    core_ref, own_ref, near_ref, far_ref, lines_ref, y_ref, z_ref, width_ref, out_ref, *grids
+    core_ref, own_ref, near_ref, far_ref, lines_ref, y_ref, z_ref, width_ref, sent_ref, *grids
 ):
+    *grids, out_ref, done = grids
+    copies = []
     partner = partners(core_ref, near_ref, far_ref)
     tables = (lines_ref, y_ref, z_ref, width_ref)
     own_plane = potentials(3, 0, *tables, grids[:3])
@@ -426,6 +428,11 @@
         out_ref[0, plane, :] = -0.5 * total
         total = mixed * own[0] + second * own[1] + (cross[2] * other[0] + cross[3] * other[1])
         out_ref[1, plane, :] = -0.5 * total
+        target = sent_ref.at[:, plane, :]
+        copies.append(pltpu.make_async_copy(out_ref.at[:, plane, :], target, done.at[x]))
+        copies[-1].start()
+    for copy in copies:
+        copy.wait()
 
 
 def own_products(refs):
@@ -471,8 +478,8 @@
     kinds += "v" * (len(args) - len(kinds))
     scratch = [pltpu.VMEM((ROWS_ALL, NG), jnp.float32) for _ in range(fields)]
     if sent:
-        scratch += [pltpu.VMEM((2 * NG, sent), jnp.float32)]
-        scratch += [pltpu.SemaphoreType.DMA((sent // LANES,))]
+        held, parts = sent
+        scratch += [pltpu.VMEM(held, jnp.float32), pltpu.SemaphoreType.DMA((parts,))]
     return pl.pallas_call(
         body,
         out_shape=jax.ShapeDtypeStruct(shape, jnp.float32),
@@ -498,22 +505,21 @@
 def ahead_own(own):
     body = functools.partial(ahead_body, 3, 0, own_products, 1)
     args = [own, *ahead_tables()]
-    return call(body, SENT_SHAPE, args, 3, 2 * 10**10, VMEM_MOST, "ahead_own", sent=OWN_LANES)
+    return call(body, SENT_SHAPE, args, 3, 2 * 10**10, VMEM_MOST, "ahead_own", sent=((2 * NG, OWN_LANES), OWN_LANES // LANES))
 
 
 def ahead_cross(core, own, near, far, ready):
     body = functools.partial(ahead_body, 4, OWN_LANES, cross_products, 5)
     args = [core, own, near, far, ready, *ahead_tables()]
-    return call(
-        body, SENT_SHAPE, args, 4, 5 * 10**9, VMEM_MOST, "ahead_cross", "svvva", CROSS_LANES
-    )
+    sent = ((2 * NG, CROSS_LANES), CROSS_LANES // LANES)
+    return call(body, SENT_SHAPE, args, 4, 5 * 10**9, VMEM_MOST, "ahead_cross", "svvva", sent)
 
 
 def back(core, own, near, far, values):
     tables = (pair(y_table().T), pair(z_back()), shared_width())
     args = [core, own, near, far, values, *(jnp.asarray(table) for table in tables)]
     shape = (2, SLAB * NG, NG)
-    return call(back_body, shape, args, 7, 5 * 10**9, VMEM_LIMIT, "back", "s")
+    return call(back_body, shape, args, 7, 5 * 10**9, VMEM_LIMIT, "back", "s", (shape, SLAB))
 
 
 def indexed(body, shapes, scalars, args, flops, name):

time: 121 us -> 120 us (level)
  no operation moved by 1% of the time
where the time goes in v5:
time: 120 us
  blocking collectives  45.8 us (38%)
  waiting for transfers between devices  28.7 us (24%)
  starting transfers between devices  27.3 us (23%)
  Pallas kernels  17 us (14%)
    all_to_all x1, blocking collectives, swap(): lax.all_to_all(blocks, 'fft', split_axis=0, concat_axis=0, tiled=True)  45.8 us
    ppermute x3, waiting for transfers between devices, body(): masks[turn_] = lax.ppermute(masks[turn_], 'fft', mask_rounds()[turn_][0])  13.4 us
    pallas_call x3, Pallas kernels, call(): pl.pallas_call(body, out_shape=jax.ShapeDtypeStruct(shape, jnp.float32),...  12.9 us
    ppermute x1, waiting for transfers between devices, body(): lax.ppermute(near, 'band', [(i, (i + 2) % count) for i in range(0, count,...  12.8 us
    all_to_all x1, starting transfers between devices, swap(): lax.all_to_all(blocks, 'fft', split_axis=0, concat_axis=0, tiled=True)  12.6 us
    ppermute x3, starting transfers between devices, body(): masks[turn_] = lax.ppermute(masks[turn_], 'fft', mask_rounds()[turn_][0])  9.21 us
    pallas_call x3, Pallas kernels, indexed(): pl.pallas_call(body, out_shape=shapes, grid_spec=pltpu.PrefetchScalarGrid...  4.05 us
    ppermute x1, starting transfers between devices, body(): lax.ppermute(near, 'band', [(i, (i + 2) % count) for i in range(0, count,...  3.54 us
  transfers between devices with their start and end apart: 6, of which 6 were waited for; matrix products, arithmetic and copies ran while one was open for 0% of the time, Pallas kernels for 5%

profile of v5, /device:TPU:44, one launch (start us, length us, event | category | flops | bytes accessed | tf_op | source)
XLA Modules:
  0.0 119.9 jit_solution(15014432161438450876)
XLA Ops:
  0.0 1.9 %collective-permute-start = (f32[2,4,128,128]{3,2,1,0:T(8,128)}, f32[2,4,128,128]{3,2,1,0:T(8,128)S(1)}, u32[]{:S(2)}, u32[]{:S(2)}) collective-permute-start(f32[2,4,128,128]{3,2,1,0:T(8,128)} %param.12), channel_id=1, source_target_pairs={{0,32},{32,0},{64,96},{96,64},{128,160},{160,128},{192,224},{224,1... | collective-permute-start | bytes 1572872 | tf_op jit(solution)/shard_map/ppermute | solution.py:572
  1.9 2.1 %collective-permute-done = f32[2,4,128,128]{3,2,1,0:T(8,128)S(1)} collective-permute-done((f32[2,4,128,128]{3,2,1,0:T(8,128)}, f32[2,4,128,128]{3,2,1,0:T(8,128)S(1)}, u32[]{:S(2)}, u32[]{:S(2)}) %collective-permute-start) | collective-permute-done | bytes 524320 | tf_op jit(solution)/shard_map/ppermute | solution.py:572
  4.0 3.5 %collective-permute-start.1 = (f32[2,4,128,128]{3,2,1,0:T(8,128)S(1)}, f32[2,4,128,128]{3,2,1,0:T(8,128)S(1)}, u32[]{:S(2)}, u32[]{:S(2)}) collective-permute-start(f32[2,4,128,128]{3,2,1,0:T(8,128)S(1)} %collective-permute-done), channel_id=1, source_target_pairs={{0,64},{64,128},{128,192},{192,256},{256,320},{320,384},{384,448},... | collective-permute-start | bytes 1572872 | tf_op jit(solution)/shard_map/ppermute | solution.py:573
  7.6 4.2 %ahead_own.1.refs_4_ = f32[256,1536]{1,0:T(8,128)} custom-call(f32[2,512,128]{2,1,0:T(8,128)} %bitcast.15, bf16[2,256,128]{2,1,0:T(8,128)(2,1)} %constant.38.clone.refs_1_.refs_5_, bf16[2,512,256]{2,1,0:T(8,128)(2,1)} %constant.39.clone.refs_2_.refs_6_, s32[256,128]{1,0:T(8,128)} %constant.40.clone.refs_3_.refs_7_.width_ref), custom_call_target="tpu_custom_call" | custom-call | flops 20000000000 | bytes 4000000 | tf_op jit(solution)/shard_map/ahead_own/pallas_call | solution.py:483
  11.8 0.0 copy-done.3
  11.8 12.8 %collective-permute-done.1 = f32[2,4,128,128]{3,2,1,0:T(8,128)S(1)} collective-permute-done((f32[2,4,128,128]{3,2,1,0:T(8,128)S(1)}, f32[2,4,128,128]{3,2,1,0:T(8,128)S(1)}, u32[]{:S(2)}, u32[]{:S(2)}) %collective-permute-start.1) | collective-permute-done | bytes 524320 | tf_op jit(solution)/shard_map/ppermute | solution.py:573
  24.6 0.8 copy-done.5
  25.4 4.8 %ahead_cross.1 = f32[256,1536]{1,0:T(8,128)} custom-call(s32[1]{0:T(128)} %bitcast.refs_0_.core_ref, f32[2,512,128]{2,1,0:T(8,128)} %bitcast.16, f32[2,512,128]{2,1,0:T(8,128)} %bitcast.18, f32[2,512,128]{2,1,0:T(8,128)} %bitcast.20, f32[256,1536]{1,0:T(8,128)} %ahead_own.1.refs_4_, ...), custom_call_target="tpu_custom_call", output_to_operand_aliasing={{}: (4, {})} | custom-call | flops 5000000000 | bytes 4000000 | tf_op jit(solution)/shard_map/ahead_cross/pallas_call | solution.py:483
  30.2 0.0 copy-start
  30.2 0.0 copy-start.1
  30.2 0.0 copy-start.11
  30.2 12.6 %all-to-all-start = ((f32[32,8,1536]{2,1,0:T(8,128)}), f32[32,8,1536]{2,1,0:T(8,128)S(1)}, u32[]{:S(2)}, u32[]{:S(2)}) async-start(f32[32,8,1536]{2,1,0:T(8,128)} %bitcast.22), calls=%async_computation | async-start | bytes 3145728 | tf_op jit(solution)/shard_map/all_to_all | solution.py:564
  42.9 0.7 mask_rows.1
  43.6 2.1 %collective-permute-start.2 = (s32[64,128]{1,0:T(8,128)S(1)}, s32[64,128]{1,0:T(8,128)S(1)}, u32[]{:S(2)}, u32[]{:S(2)}) collective-permute-start(s32[64,128]{1,0:T(8,128)S(1)} %get-tuple-element.14), channel_id=1, source_target_pairs={{8,0},{9,1},{10,2},{11,3},{12,4},{13,5},{14,6},{15,7},{0,8},{1,9},... | collective-permute-start | bytes 98312 | tf_op jit(solution)/shard_map/ppermute | solution.py:582
  45.7 4.6 %collective-permute-start.3 = (s32[64,128]{1,0:T(8,128)S(1)}, s32[64,128]{1,0:T(8,128)S(1)}, u32[]{:S(2)}, u32[]{:S(2)}) collective-permute-start(s32[64,128]{1,0:T(8,128)S(1)} %get-tuple-element.15), channel_id=1, source_target_pairs={{16,0},{17,1},{18,2},{19,3},{20,4},{21,5},{22,6},{23,7},{24,8},{25... | collective-permute-start | bytes 98312 | tf_op jit(solution)/shard_map/ppermute | solution.py:582
  50.3 2.5 %collective-permute-start.4 = (s32[64,128]{1,0:T(8,128)S(1)}, s32[64,128]{1,0:T(8,128)S(1)}, u32[]{:S(2)}, u32[]{:S(2)}) collective-permute-start(s32[64,128]{1,0:T(8,128)S(1)} %get-tuple-element.16), channel_id=1, source_target_pairs={{24,0},{25,1},{26,2},{27,3},{28,4},{29,5},{30,6},{31,7},{16,8},{17... | collective-permute-start | bytes 98312 | tf_op jit(solution)/shard_map/ppermute | solution.py:582
  52.8 4.8 %collective-permute-done.2.rest_1_ = s32[64,128]{1,0:T(8,128)S(1)} collective-permute-done((s32[64,128]{1,0:T(8,128)S(1)}, s32[64,128]{1,0:T(8,128)S(1)}, u32[]{:S(2)}, u32[]{:S(2)}) %collective-permute-start.2) | collective-permute-done | bytes 32800 | tf_op jit(solution)/shard_map/ppermute | solution.py:582
  57.6 5.8 %collective-permute-done.3.rest_2_ = s32[64,128]{1,0:T(8,128)S(1)} collective-permute-done((s32[64,128]{1,0:T(8,128)S(1)}, s32[64,128]{1,0:T(8,128)S(1)}, u32[]{:S(2)}, u32[]{:S(2)}) %collective-permute-start.3) | collective-permute-done | bytes 32800 | tf_op jit(solution)/shard_map/ppermute | solution.py:582
  63.5 2.8 %collective-permute-done.4.rest_3_ = s32[64,128]{1,0:T(8,128)S(1)} collective-permute-done((s32[64,128]{1,0:T(8,128)S(1)}, s32[64,128]{1,0:T(8,128)S(1)}, u32[]{:S(2)}, u32[]{:S(2)}) %collective-permute-start.4) | collective-permute-done | bytes 32800 | tf_op jit(solution)/shard_map/ppermute | solution.py:582
  66.3 0.8 weights.1.weight_ref
  67.1 0.4 all-to-all-done
  67.5 2.5 %middle.1 = f32[256,1536]{1,0:T(8,128)S(1)} custom-call(s32[1]{0:T(128)} %bitcast.4.me_ref, f32[256,1536]{1,0:T(8,128)S(1)} %bitcast.11, f32[256,256]{1,0:T(8,128)S(1)} %weights.1.weight_ref, bf16[2,512,256]{2,1,0:T(8,128)(2,1)S(1)} %copy-done.8), custom_call_target="tpu_custom_call" | custom-call | flops 4000000000 | bytes 2000000 | tf_op jit(solution)/shard_map/middle/pallas_call | solution.py:527
  70.1 0.0 copy-start.2
  70.1 0.0 copy-start.4
  70.1 0.0 copy-start.7
  70.1 0.0 copy-start.9
  70.1 0.0 copy-start.10
  70.2 45.8 %all_to_all.10 = f32[32,8,1536]{2,1,0:T(8,128)S(1)} all-to-all(f32[32,8,1536]{2,1,0:T(8,128)S(1)} %bitcast.13), channel_id=1, replica_groups=mesh['band'=16,'fft'=32] {'fft'}, dimensions={0} | all-to-all | bytes 3145728 | tf_op jit(solution)/shard_map/all_to_all | solution.py:564
  116.0 0.0 copy-done.7
  116.0 0.0 copy-done.9
  116.0 0.0 copy-done.10
  116.0 3.9 %back.1 = f32[2,512,128]{2,1,0:T(8,128)} custom-call(s32[1]{0:T(128)} %bitcast.refs_0_.core_ref, f32[2,512,128]{2,1,0:T(8,128)S(1)} %bitcast.17, f32[2,512,128]{2,1,0:T(8,128)S(1)} %bitcast.19, f32[2,512,128]{2,1,0:T(8,128)S(1)} %bitcast.21, f32[256,1536]{1,0:T(8,128)S(1)} %bitcast.12, bf16[2,128,256]{2,1,0:T(8,128)(2,1)S(1)} %copy-done.10, ...), custom_call_target="tpu_custom_call" | custom-call | flops 5000000000 | bytes 4000000 | tf_op jit(solution)/shard_map/back/pallas_call | solution.py:483
  (11 shorter events, 0.0 us)
Async XLA Ops:
  0.0 4.0 %collective-permute-start = (f32[2,4,128,128]{3,2,1,0:T(8,128)}, f32[2,4,128,128]{3,2,1,0:T(8,128)S(1)}, u32[]{:S(2)}, u32[]{:S(2)}) collective-permute-start(f32[2,4,128,128]{3,2,1,0:T(8,128)} %param.12), channel_id=1, source_target_pairs={{0,32},{32,0},{64,96},{96,64},{128,160},{160,128},{192,224},{224,1... | collective-permute-start | bytes 1572872 | tf_op jit(solution)/shard_map/ppermute | solution.py:572
  4.0 7.8 %copy-start.3 = (f32[2,4,128,128]{3,2,1,0:T(8,128)}, f32[2,4,128,128]{3,2,1,0:T(8,128)S(1)}, u32[]{:S(2)}) copy-start(f32[2,4,128,128]{3,2,1,0:T(8,128)S(1)} %collective-permute-done) | copy-start | bytes 1572868
  4.0 20.6 %collective-permute-start.1 = (f32[2,4,128,128]{3,2,1,0:T(8,128)S(1)}, f32[2,4,128,128]{3,2,1,0:T(8,128)S(1)}, u32[]{:S(2)}, u32[]{:S(2)}) collective-permute-start(f32[2,4,128,128]{3,2,1,0:T(8,128)S(1)} %collective-permute-done), channel_id=1, source_target_pairs={{0,64},{64,128},{128,192},{192,256},{256,320},{320,384},{384,448},... | collective-permute-start | bytes 1572872 | tf_op jit(solution)/shard_map/ppermute | solution.py:573
  24.6 0.8 copy-start.5
  30.2 12.7 %copy-start = (s32[128,4,128]{2,1,0:T(4,128)S(1)}, s32[128,4,128]{2,1,0:T(4,128)}, u32[]{:S(2)}) copy-start(s32[128,4,128]{2,1,0:T(4,128)} %param.13) | copy-start | bytes 786436
  30.2 12.7 %copy-start.1 = (s32[512]{0:T(512)S(1)}, s32[512]{0:T(512)}, u32[]{:S(2)}) copy-start(s32[512]{0:T(512)} %constant.41.clone.device_ref) | copy-start | bytes 6148
  30.2 36.0 %copy-start.11 = (s32[8,256]{1,0:T(8,128)S(1)}, s32[8,256]{1,0:T(8,128)}, u32[]{:S(2)}) copy-start(s32[8,256]{1,0:T(8,128)} %constant.42.clone.lane_ref) | copy-start | bytes 24580
  30.2 37.3 %all-to-all-start = ((f32[32,8,1536]{2,1,0:T(8,128)}), f32[32,8,1536]{2,1,0:T(8,128)S(1)}, u32[]{:S(2)}, u32[]{:S(2)}) async-start(f32[32,8,1536]{2,1,0:T(8,128)} %bitcast.22), calls=%async_computation | async-start | bytes 3145728 | tf_op jit(solution)/shard_map/all_to_all | solution.py:564
  43.6 14.1 %collective-permute-start.2 = (s32[64,128]{1,0:T(8,128)S(1)}, s32[64,128]{1,0:T(8,128)S(1)}, u32[]{:S(2)}, u32[]{:S(2)}) collective-permute-start(s32[64,128]{1,0:T(8,128)S(1)} %get-tuple-element.14), channel_id=1, source_target_pairs={{8,0},{9,1},{10,2},{11,3},{12,4},{13,5},{14,6},{15,7},{0,8},{1,9},... | collective-permute-start | bytes 98312 | tf_op jit(solution)/shard_map/ppermute | solution.py:582
  45.7 17.8 %collective-permute-start.3 = (s32[64,128]{1,0:T(8,128)S(1)}, s32[64,128]{1,0:T(8,128)S(1)}, u32[]{:S(2)}, u32[]{:S(2)}) collective-permute-start(s32[64,128]{1,0:T(8,128)S(1)} %get-tuple-element.15), channel_id=1, source_target_pairs={{16,0},{17,1},{18,2},{19,3},{20,4},{21,5},{22,6},{23,7},{24,8},{25... | collective-permute-start | bytes 98312 | tf_op jit(solution)/shard_map/ppermute | solution.py:582
  50.3 15.9 %collective-permute-start.4 = (s32[64,128]{1,0:T(8,128)S(1)}, s32[64,128]{1,0:T(8,128)S(1)}, u32[]{:S(2)}, u32[]{:S(2)}) collective-permute-start(s32[64,128]{1,0:T(8,128)S(1)} %get-tuple-element.16), channel_id=1, source_target_pairs={{24,0},{25,1},{26,2},{27,3},{28,4},{29,5},{30,6},{31,7},{16,8},{17... | collective-permute-start | bytes 98312 | tf_op jit(solution)/shard_map/ppermute | solution.py:582
  66.3 1.3 %copy-start.8 = (bf16[2,512,256]{2,1,0:T(8,128)(2,1)S(1)}, bf16[2,512,256]{2,1,0:T(8,128)(2,1)}, u32[]{:S(2)}) copy-start(bf16[2,512,256]{2,1,0:T(8,128)(2,1)} %constant.43.clone.table_ref) | copy-start | bytes 1572868
  70.1 45.9 %copy-start.2 = (f32[2,4,128,128]{3,2,1,0:T(8,128)S(1)}, f32[2,4,128,128]{3,2,1,0:T(8,128)}, u32[]{:S(2)}) copy-start(f32[2,4,128,128]{3,2,1,0:T(8,128)} %param.12) | copy-start | bytes 1572868
  70.1 45.9 %copy-start.4 = (f32[2,4,128,128]{3,2,1,0:T(8,128)S(1)}, f32[2,4,128,128]{3,2,1,0:T(8,128)}, u32[]{:S(2)}) copy-start(f32[2,4,128,128]{3,2,1,0:T(8,128)} %copy-done.3) | copy-start | bytes 1572868
  70.1 45.9 %copy-start.6 = (f32[2,4,128,128]{3,2,1,0:T(8,128)S(1)}, f32[2,4,128,128]{3,2,1,0:T(8,128)}, u32[]{:S(2)}) copy-start(f32[2,4,128,128]{3,2,1,0:T(8,128)} %copy-done.5) | copy-start | bytes 1572868
  70.1 45.9 %copy-start.7 = (bf16[2,512,256]{2,1,0:T(8,128)(2,1)S(1)}, bf16[2,512,256]{2,1,0:T(8,128)(2,1)}, u32[]{:S(2)}) copy-start(bf16[2,512,256]{2,1,0:T(8,128)(2,1)} %constant.45.clone.z_ref) | copy-start | bytes 1572868
  70.1 45.9 %copy-start.9 = (s32[256,128]{1,0:T(8,128)S(1)}, s32[256,128]{1,0:T(8,128)}, u32[]{:S(2)}) copy-start(s32[256,128]{1,0:T(8,128)} %constant.40.clone.refs_3_.refs_7_.width_ref) | copy-start | bytes 393220
  70.1 45.9 %copy-start.10 = (bf16[2,128,256]{2,1,0:T(8,128)(2,1)S(1)}, bf16[2,128,256]{2,1,0:T(8,128)(2,1)}, u32[]{:S(2)}) copy-start(bf16[2,128,256]{2,1,0:T(8,128)(2,1)} %constant.44.clone.y_ref) | copy-start | bytes 393220
